TPU v7x, 32 devices: a whole 2x2x4 slice. The times are simulated.
32 devices in a mesh: rows: 16 (over z, y, x), rep: 2 (over core).
Axes of the slice: x: 2, y: 2, z: 4, core: 2. Of those that a mesh axis runs over, the one named last changes fastest.
Arguments:
- nodes: bfloat16 [2048, 512], P('rows'), may hold values from -6 to 6
- adjacency: bfloat16 [2048, 2048], P('rows', 'rep'), may hold values from 0 to 2, as said below
- gain: float32 [512], replicated, may hold values from 0.1 to 1.9
- w_in: bfloat16 [512, 512], replicated, may hold values from -0.25 to 0.25
- w_out: bfloat16 [512, 512], replicated, may hold values from -0.25 to 0.25
- cotangent: bfloat16 [2048, 512], P('rows'), may hold values from -2 to 2
Outputs:
- node_out: bfloat16 [2048, 512], P('rows')
- node_grad: bfloat16 [2048, 512], P('rows')
- grad_w_in: float32 [512, 512], replicated
- grad_w_out: float32 [512, 512], replicated
- grad_gain: float32 [512], replicated
Inputs may be any that keep to these rules, and one draw needn't show every extreme that they name: adjacency holds whole numbers, is symmetric, every diagonal entry is 1, and off the diagonal it is zero outside a set of live 128 x 128 blocks.
All inputs are finite; a program needn't handle non-finite values.
Results may differ from a plain program's by a relative error of at most 0.0054.
Values may be sent and summed in bfloat16 or wider, within the bound.
A program may use at most 64 MiB of HBM per device.

v0:
```python
import jax
import jax.numpy as jnp
from jax import lax
from jax.sharding import PartitionSpec as P


def broadcast(x, axis, root):
    mine = lax.axis_index(axis) == root
    return lax.psum(jnp.where(mine, x, jnp.zeros_like(x)), axis)


def aggregate(strip_half, field):
    owners = lax.axis_size("rows") // lax.axis_size("rep")
    group = field.shape[0]
    first_owner = lax.axis_index("rep") * owners
    total = jnp.zeros((group, field.shape[1]), jnp.float32)
    for step in range(owners):
        owner_block = broadcast(field, "rows", first_owner + step)
        columns = strip_half[:, step * group : (step + 1) * group]
        total = total + jnp.dot(columns, owner_block, preferred_element_type=jnp.float32)
    return total


def node_update(summed, nodes, cotangent, gain, w_in, w_out):
    scale = lax.rsqrt(jnp.mean(summed * summed, axis=-1, keepdims=True) + 1e-05)
    normed = summed * scale
    lifted = (normed * gain).astype(jnp.bfloat16)
    pre = jnp.dot(lifted, w_in, preferred_element_type=jnp.float32)
    sigma = jax.nn.sigmoid(pre)
    hidden = (pre * sigma).astype(jnp.bfloat16)
    node_out = (
        nodes.astype(jnp.float32) + jnp.dot(hidden, w_out, preferred_element_type=jnp.float32)
    ).astype(jnp.bfloat16)
    grad_hidden = jnp.dot(cotangent, w_out.T, preferred_element_type=jnp.float32)
    grad_pre = (grad_hidden * sigma * (1.0 + pre * (1.0 - sigma))).astype(jnp.bfloat16)
    grad_w_out = jnp.dot(hidden.T, cotangent, preferred_element_type=jnp.float32)
    grad_w_in = jnp.dot(lifted.T, grad_pre, preferred_element_type=jnp.float32)
    grad_lifted = jnp.dot(grad_pre, w_in.T, preferred_element_type=jnp.float32)
    grad_gain = jnp.sum(grad_lifted * normed, axis=0)
    grad_normed = grad_lifted * gain
    grad_summed = (
        scale * (grad_normed - normed * jnp.mean(grad_normed * normed, axis=-1, keepdims=True))
    ).astype(jnp.bfloat16)
    return (node_out, grad_summed, grad_w_in, grad_w_out, grad_gain)


def shards(nodes, adjacency, gain, w_in, w_out, cotangent):
    partial_value = aggregate(adjacency, nodes)

    def reduce_full(terms):
        return lax.psum(terms, "rep")

    summed = reduce_full(partial_value)
    node_out, grad_summed, grad_w_in, grad_w_out, grad_gain = node_update(
        summed, nodes, cotangent, gain, w_in, w_out
    )
    back_full = reduce_full(aggregate(adjacency, grad_summed))
    node_grad = (cotangent.astype(jnp.float32) + back_full).astype(jnp.bfloat16)
    grad_w_in, grad_w_out, grad_gain = lax.psum((grad_w_in, grad_w_out, grad_gain), "rows")
    return (node_out, node_grad, grad_w_in, grad_w_out, grad_gain)


def solution(mesh):
    return jax.shard_map(
        shards,
        mesh=mesh,
        in_specs=(P("rows", None), P("rows", "rep"), P(), P(), P(), P("rows", None)),
        out_specs=(P("rows", None), P("rows", None), P(), P(), P()),
        check_vma=False,
    )
```

profile of v0, /device:TPU:1, one launch (start us, length us, event | category | flops | bytes accessed | tf_op | source)
XLA Modules:
  0.0 448.5 jit_solution(12406967560336825084)
XLA Ops:
  7.2 1.1 copy.11
  8.3 1.0 broadcast_select_fusion.1
  9.4 121.5 %all-reduce.17.cloned.1.call-done = (bf16[128,512]{0,1:T(8,128)(2,1)}, bf16[128,512]{0,1:T(8,128)(2,1)}, bf16[128,512]{0,1:T(8,128)(2,1)}, bf16[128,512]{0,1:T(8...) async-done(((bf16[128,512]{0,1:T(8,128)(2,1)}, bf16[128,512]{0,1:T(8,128)(2,1)}, ...) | async-done | bytes 1048592 | tf_op jit(solution)/shard_map/psum | solution.py:9
  130.8 1.1 fusion.21
  133.1 0.7 copy-done.14
  135.8 0.7 copy-done.8
  137.4 0.9 fusion.1
  138.4 18.3 %all-reduce.9.cloned.1.call-done = f32[128,512]{0,1:T(8,128)} async-done(((f32[128,512]{0,1:T(8,128)}), f32[128,512]{0,1:T(8,128)}) %all-reduce.9.cloned.1.call-update) | async-done | bytes 262160 | tf_op jit(solution)/shard_map/psum | solution.py:51
  156.7 1.1 multiply_reduce_fusion.2
  159.7 0.8 broadcast_select_fusion
  160.5 0.9 broadcast_select_fusion.2
  161.5 117.9 %all-reduce.15.cloned.1.call-done = (bf16[128,512]{0,1:T(8,128)(2,1)}, bf16[128,512]{0,1:T(8,128)(2,1)}, bf16[128,512]{0,1:T(8,128)(2,1)}, bf16[128,512]{0,1:T(8...) async-done(((bf16[128,512]{0,1:T(8,128)(2,1)}, bf16[128,512]{0,1:T(8,128)(2,1)}, ...) | async-done | bytes 1048592 | tf_op jit(solution)/shard_map/psum | solution.py:9
  279.4 1.1 fusion.19
  284.3 0.7 copy-done.9
  285.9 0.9 fusion
  286.9 1.3 fusion.25
  288.2 1.3 fusion.23
  289.7 33.3 %psum.167 = f32[512]{0:T(512)} all-reduce(f32[512]{0:T(512)S(1)} %get-tuple-element.10), channel_id=1, replica_groups=mesh['rows'=16,'rep'=2] {'rows'}, use_global_device_ids=true, to_apply=%region_23.24 | all-reduce | flops 512 | bytes 4096 | tf_op jit(solution)/shard_map/psum | solution.py:59
  323.0 0.9 fusion.3
  323.9 1.0 add_convert_fusion
  324.9 0.8 copy.22
  325.6 113.0 %all-reduce.13.cloned.1.call-done = (f32[512,512]{1,0:T(8,128)}, f32[512,512]{1,0:T(8,128)}) async-done(((f32[512,512]{1,0:T(8,128)}, f32[512,512]{1,0:T(8,128)}), (f32[512,512]{1,0:T(8,128)}, f32[512,512]{1,0:T(8,128)})) %all-reduce.13.cloned.1.call-update) | async-done | bytes 2097168 | tf_op jit(solution)/shard_map/psum | solution.py:59
  438.6 2.4 copy.44
  441.0 1.0 copy.45
  (70 shorter events, 10.9 us)
Async XLA Ops:
  7.2 150.7 %copy-start = (bf16[512,512]{1,0:T(8,128)(2,1)S(1)}, bf16[512,512]{1,0:T(8,128)(2,1)}, u32[]{:S(2)}) copy-start(bf16[512,512]{1,0:T(8,128)(2,1)} %param.9) | copy-start | bytes 1572868
  7.2 123.7 %all-reduce.17.cloned.1.call-start = ((), (), s32[]{:S(2)}) async-start(), calls=%async_computation.4 | async-start | bytes 2097152 | tf_op jit(solution)/shard_map/psum | solution.py:9
  9.3 121.5 %copy-start.3 = (bf16[128,1024]{1,0:T(8,128)(2,1)S(1)}, bf16[128,1024]{1,0:T(8,128)(2,1)}, u32[]{:S(2)}) copy-start(bf16[128,1024]{1,0:T(8,128)(2,1)} %param.7) | copy-start | bytes 786436
  9.3 147.4 %all-reduce.9.cloned.1.call-start = ((), (), s32[]{:S(2)}) async-start(), calls=%async_computation | async-start | bytes 524288 | tf_op jit(solution)/shard_map/psum | solution.py:51
  130.8 1.1 copy-start.18
  132.0 0.9 copy-start.16
  132.9 0.9 copy-start.14
  133.8 0.9 copy-start.12
  134.7 0.9 copy-start.10
  135.6 0.9 copy-start.8
  136.5 0.9 copy-start.6
  138.3 141.1 %all-reduce.15.cloned.1.call-start = ((), (), s32[]{:S(2)}) async-start(), calls=%async_computation.3 | async-start | bytes 2097152 | tf_op jit(solution)/shard_map/psum | solution.py:9
  156.7 1.1 copy-start.1
  156.7 1.1 copy-start.20
  157.8 0.9 copy-start.4
  157.9 1.1 copy-start.21
  161.4 162.5 %all-reduce.11.cloned.1.call-start = ((), (), s32[]{:S(2)}) async-start(), calls=%async_computation.1 | async-start | bytes 524288 | tf_op jit(solution)/shard_map/psum | solution.py:51
  279.4 1.1 copy-start.19
  280.5 0.9 copy-start.17
  281.4 0.9 copy-start.15
  285.0 0.9 copy-start.7
  286.9 151.8 %all-reduce.13.cloned.1.call-start = ((), (), s32[]{:S(2)}) async-start(), calls=%async_computation.2 | async-start | bytes 4194304 | tf_op jit(solution)/shard_map/psum | solution.py:59
  289.5 33.4 %copy-start.5 = (bf16[128,512]{1,0:T(8,128)(2,1)S(1)}, bf16[128,512]{1,0:T(8,128)(2,1)}, u32[]{:S(2)}) copy-start(bf16[128,512]{1,0:T(8,128)(2,1)} %param.6) | copy-start | bytes 393220
  438.6 2.4 copy-start.2
  (3 other events, 2.7 us)
Sparse Core Ops, SparseCore 0:
  14.7 116.0 all-reduce.16
  138.4 18.2 all-reduce.8
  164.5 114.8 all-reduce.14
  287.0 18.2 all-reduce.10
  311.2 127.3 all-reduce.12
where the time goes:
time: 449 us; the launch traced here: 448 us
  waiting for transfers between devices  371 us (83%)
  blocking collectives  33.3 us (7%)
  local copies, waits for them, and re-layouts  14.5 us (3%)
  between operations  14.1 us (3%)
  matrix products  10.9 us (2%)
  other arithmetic  4.78 us (1%)
    psum x2, waiting for transfers between devices, broadcast(): return lax.psum(jnp.where(mine, x, jnp.zeros_like(x)), axis)  239 us
    psum x1, waiting for transfers between devices, shards(): lax.psum((grad_w_in, grad_w_out, grad_gain), 'rows')  113 us
    psum x1, blocking collectives, shards(): lax.psum((grad_w_in, grad_w_out, grad_gain), 'rows')  33.3 us
    psum x2, waiting for transfers between devices, reduce_full(): return lax.psum(terms, 'rep')  18.3 us
    unnamed x49, local copies, waits for them, and re-layouts  14.5 us
  transfers between devices with their start and end apart: 5, of which 4 were waited for; matrix products, arithmetic and copies ran while one was open for 1% of the time, Pallas kernels for 0%

commit v1 on v0

v1 whole, which is shorter than its diff:
```python
import functools
import math

import jax
import jax.numpy as jnp
from jax import lax
from jax.experimental import pallas as pl
from jax.experimental.pallas import tpu as pltpu
from jax.sharding import PartitionSpec as P

MESH = pl.DeviceIdType.MESH
F32 = jnp.float32
BF16 = jnp.bfloat16


def dot(a, b, ca=1, cb=0):
    return lax.dot_general(a, b, (((ca,), (cb,)), ((), ())), preferred_element_type=F32)


def kernel(
    Z, PL, C, spread,
    nodes_h, adj_h, gain_ref, w_in_h, w_out_h, cot_h,
    node_out_ref, node_grad_ref, gw_ref, gg_ref,
    nodes, w_in, w_out, cot, a2, x, x2,
    part, cin, acc, pin, full, part2, cin2, acc2, pin2, full2,
    gs, lh, rh, gpart, gin, gz, gzin, gw, gg, ggp, ggz,
    loc, a_s, a_r, x_s, x_r, x2_s, x2_r,
    c_s, c_r, p_s, p_r, f_s, f_r, c2_s, c2_r, p2_s, p2_r, f2_s, f2_r,
    g_s, g_r, z_s, z_r, zg_s, zg_r, pg_s, pg_r, rg_s, rg_r,
    ggp_s, ggp_r, ggz_s, ggz_r,
):
    g = lax.axis_index("rows")
    r = lax.axis_index("rep")
    z, p = lax.div(g, PL), lax.rem(g, PL)
    ppr = Z // C
    group, D = nodes.shape
    pc = group // C
    rows_w = 2 * D // C
    w1 = rows_w // PL
    zl = lax.rem(z, ppr)
    owner = lax.div(z, ppr) == r
    sends = []

    def z_peer(d):
        return {"rows": lax.rem(z + d, Z) * PL + p}

    def p_peer(d):
        return {"rows": z * PL + lax.rem(p + d, PL)}

    def r_peer(d):
        return {"rep": lax.rem(r + d, C)}

    def rcopy(src, dst, ss, rs, dev):
        return pltpu.make_async_remote_copy(
            src_ref=src, dst_ref=dst, send_sem=ss, recv_sem=rs, device_id=dev, device_id_type=MESH
        )

    def send(src, dst, ss, rs, dev):
        c = rcopy(src, dst, ss, rs, dev)
        c.start()
        sends.append(c)

    def arrived(dst, ss, rs, dev):
        rcopy(dst, dst, ss, rs, dev).wait_recv()

    own_cols = [
        pltpu.make_async_copy(
            adj_h.at[:, pl.ds(pl.multiple_of((k * PL + p) * group, group), group)],
            a2.at[pl.ds(pl.multiple_of(p * group, group), group), pl.ds(k * group, group)],
            loc.at[4 + k],
        )
        for k in range(ppr)
    ]
    loads = [
        pltpu.make_async_copy(cot_h, cot, loc.at[0]),
        pltpu.make_async_copy(w_out_h, w_out, loc.at[1]),
        pltpu.make_async_copy(w_in_h, w_in, loc.at[2]),
        pltpu.make_async_copy(nodes_h, nodes, loc.at[3]),
    ]
    loads[3].start()
    for c in own_cols:
        c.start()
    for c in loads[:3]:
        c.start()

    barrier = pltpu.get_barrier_semaphore()
    for n, peer in ((Z, z_peer), (PL, p_peer), (C, r_peer)):
        for d in range(1, n):
            pl.semaphore_signal(barrier, inc=1, device_id=peer(d), device_id_type=MESH)
    loads[3].wait()
    pl.semaphore_wait(barrier, Z + PL + C - 3)

    def z_copies(src, buf, ss, rs):
        slot = buf.at[pl.ds(pl.multiple_of(zl * group, group), group)]
        return [rcopy(src, slot, ss.at[d - 1], rs.at[zl], z_peer(d)) for d in range(1, Z)]

    def z_start(src, buf, ss, rs):
        @pl.when(owner)
        def _():
            for c in z_copies(src, buf, ss, rs):
                c.start()
            buf[pl.ds(pl.multiple_of(zl * group, group), group)] = src[...]

    def z_wait(src, buf, ss, rs):
        for k in range(ppr):
            @pl.when(r * ppr + k != z)
            def _():
                arrived(buf.at[pl.ds(k * group, group)], ss.at[0], rs.at[k], z_peer(1))

    def z_drain(src, buf, ss, rs):
        @pl.when(owner)
        def _():
            for c in z_copies(src, buf, ss, rs):
                c.wait_send()

    z_start(nodes, x, x_s, x_r)
    for d in range(1, PL):
        q = lax.rem(p + d, PL)
        for k in range(ppr):
            send(
                adj_h.at[:, pl.ds(pl.multiple_of((k * PL + q) * group, group), group)],
                a2.at[pl.ds(pl.multiple_of(p * group, group), group), pl.ds(k * group, group)],
                a_s.at[(d - 1) * ppr + k], a_r.at[(d - 1) * ppr + k], p_peer(d),
            )

    loads[0].wait()
    loads[1].wait()
    grad_hidden = dot(cot[...], w_out[...], 1, 1)
    loads[2].wait()
    for c in own_cols:
        c.wait()
    for d in range(1, PL):
        q = lax.rem(p + PL - d, PL)
        for k in range(ppr):
            arrived(
                a2.at[pl.ds(pl.multiple_of(q * group, group), group), pl.ds(k * group, group)],
                a_s.at[(d - 1) * ppr + k], a_r.at[(d - 1) * ppr + k], p_peer(d),
            )

    def partials(buf, out, ins, ss, rs):
        for q in range(PL):
            val = dot(a2[q * group:(q + 1) * group], buf[...])
            for c in range(C):
                out[c, q] = val[c * pc:(c + 1) * pc].astype(out.dtype)
        for d in range(1, C):
            send(out.at[lax.rem(r + d, C)], ins.at[d - 1], ss.at[d - 1], rs.at[d - 1], r_peer(d))

    def combine(out, ins, ss, rs, accs, pins, pss, prs):
        for d in range(1, C):
            arrived(ins.at[d - 1], ss.at[d - 1], rs.at[d - 1], r_peer(d))
        for d in list(range(1, PL)) + [0]:
            q = lax.rem(p + d, PL)
            val = out[r, q].astype(F32)
            for e in range(C - 1):
                val = val + ins[e, q].astype(F32)
            if d == 0:
                return val
            accs[d - 1] = val.astype(accs.dtype)
            send(accs.at[d - 1], pins.at[d - 1], pss.at[d - 1], prs.at[d - 1], p_peer(d))

    def finish(val, accs, pins, pss, prs):
        for d in range(1, PL):
            arrived(pins.at[d - 1], pss.at[d - 1], prs.at[d - 1], p_peer(d))
            val = val + pins[d - 1].astype(F32)
        return val

    def piece_of(buf, c):
        return buf.at[pl.ds(pl.multiple_of(c * pc, pc), pc)]

    def share(buf, ss, rs):
        for d in range(1, C):
            send(piece_of(buf, r), piece_of(buf, r), ss.at[d - 1], rs.at[d - 1], r_peer(d))

    def shared(buf, ss, rs):
        for d in range(1, C):
            arrived(piece_of(buf, lax.rem(r + C - d, C)), ss.at[d - 1], rs.at[d - 1], r_peer(d))

    mine = pl.ds(pl.multiple_of(r * pc, pc), pc)
    z_wait(nodes, x, x_s, x_r)
    partials(x, part, cin, c_s, c_r)
    own = combine(part, cin, c_s, c_r, acc, pin, p_s, p_r)
    full[mine] = finish(own, acc, pin, p_s, p_r)
    share(full, f_s, f_r)
    shared(full, f_s, f_r)

    summed = full[...]
    gain = gain_ref[...]
    scale = lax.rsqrt(jnp.mean(summed * summed, axis=-1, keepdims=True) + 1e-05)
    normed = summed * scale
    lifted = (normed * gain).astype(BF16)
    pre = dot(lifted, w_in[...])
    sigma = jax.nn.sigmoid(pre)
    hidden = (pre * sigma).astype(BF16)
    grad_pre = (grad_hidden * sigma * (1.0 + pre * (1.0 - sigma))).astype(BF16)
    grad_lifted = dot(grad_pre, w_in[...], 1, 1)
    grad_normed = grad_lifted * gain
    gs[...] = (
        scale * (grad_normed - normed * jnp.mean(grad_normed * normed, axis=-1, keepdims=True))
    ).astype(BF16)
    z_start(gs, x2, x2_s, x2_r)

    lh[0] = lifted
    lh[1] = hidden
    rh[0] = grad_pre
    rh[1] = cot[...]
    half = C // 2
    which = lax.div(r, half)
    first = lax.rem(r, half) * rows_w
    left = lh[which, :, pl.ds(pl.multiple_of(first, rows_w), rows_w)] if half > 1 else lh[which]
    gval = dot(left, rh[which], 0, 0)
    for q in range(PL):
        gpart[q] = gval[q * w1:(q + 1) * w1].astype(BF16)
    for d in range(1, PL):
        send(gpart.at[lax.rem(p + d, PL)], gin.at[d - 1], g_s.at[d - 1], g_r.at[d - 1], p_peer(d))
    gg[...] = jnp.broadcast_to(jnp.sum(grad_lifted * normed, axis=0, keepdims=True), gg.shape)
    ggp[p] = gg[...]
    for d in range(1, PL):
        send(gg, ggp.at[p], ggp_s.at[d - 1], ggp_r.at[d - 1], p_peer(d))
    node_out_ref[...] = (nodes[...].astype(F32) + dot(hidden, w_out[...])).astype(BF16)

    z_wait(gs, x2, x2_s, x2_r)
    partials(x2, part2, cin2, c2_s, c2_r)

    gsum = gpart[p].astype(F32)
    for d in range(1, PL):
        arrived(gin.at[d - 1], g_s.at[d - 1], g_r.at[d - 1], p_peer(d))
        gsum = gsum + gin[d - 1].astype(F32)
    base = r * rows_w + p * w1
    if spread:
        wz = w1 // Z
        for k in range(Z):
            gz[k] = gsum[k * wz:(k + 1) * wz].astype(BF16)
        for d in range(1, Z):
            send(gz.at[lax.rem(z + d, Z)], gzin.at[d - 1], z_s.at[d - 1], z_r.at[d - 1], z_peer(d))
    else:
        gz[0] = gsum.astype(BF16)
        gzin[z] = gz[0]
        for d in range(1, Z):
            send(gz.at[0], gzin.at[z], z_s.at[d - 1], z_r.at[d - 1], z_peer(d))

    for d in range(1, PL):
        arrived(ggp.at[lax.rem(p + PL - d, PL)], ggp_s.at[d - 1], ggp_r.at[d - 1], p_peer(d))
    ggv = ggp[0]
    for q in range(1, PL):
        ggv = ggv + ggp[q]
    ggz[z] = ggv
    for d in range(1, Z):
        send(ggz.at[z], ggz.at[z], ggz_s.at[d - 1], ggz_r.at[d - 1], z_peer(d))

    own2 = combine(part2, cin2, c2_s, c2_r, acc2, pin2, p2_s, p2_r)

    def gw_rows(start, count):
        return gw.at[pl.ds(pl.multiple_of(start, count), count)]

    if spread:
        shard = gz[z].astype(F32)
        for d in range(1, Z):
            arrived(gzin.at[d - 1], z_s.at[d - 1], z_r.at[d - 1], z_peer(d))
            shard = shard + gzin[d - 1].astype(F32)
        here = base + z * wz
        gw[pl.ds(pl.multiple_of(here, wz), wz)] = shard.astype(BF16)
        for d in range(1, Z):
            send(gw_rows(here, wz), gw_rows(here, wz), zg_s.at[d - 1], zg_r.at[d - 1], z_peer(d))
    else:
        for d in range(1, Z):
            arrived(gzin.at[lax.rem(z + Z - d, Z)], z_s.at[d - 1], z_r.at[d - 1], z_peer(d))
        shard = gzin[0].astype(F32)
        for k in range(1, Z):
            shard = shard + gzin[k].astype(F32)
        gw[pl.ds(pl.multiple_of(base, w1), w1)] = shard.astype(BF16)

    back = finish(own2, acc2, pin2, p2_s, p2_r)
    full2[mine] = (cot[mine].astype(F32) + back).astype(BF16)
    share(full2, f2_s, f2_r)

    if spread:
        for d in range(1, Z):
            there = base + lax.rem(z + Z - d, Z) * wz
            arrived(gw_rows(there, wz), zg_s.at[d - 1], zg_r.at[d - 1], z_peer(d))
    for d in range(1, PL):
        send(gw_rows(base, w1), gw_rows(base, w1), pg_s.at[d - 1], pg_r.at[d - 1], p_peer(d))
    for d in range(PL):
        q = lax.rem(p + PL - d, PL)
        block = gw_rows(r * rows_w + q * w1, w1)
        if d > 0:
            arrived(block, pg_s.at[d - 1], pg_r.at[d - 1], p_peer(d))
        for e in range(1, C):
            i = d * (C - 1) + e - 1
            send(block, block, rg_s.at[i], rg_r.at[i], r_peer(e))

    for d in range(1, Z):
        arrived(ggz.at[lax.rem(z + Z - d, Z)], ggz_s.at[d - 1], ggz_r.at[d - 1], z_peer(d))
    ggv = ggz[0]
    for k in range(1, Z):
        ggv = ggv + ggz[k]
    gg_ref[...] = ggv
    shared(full2, f2_s, f2_r)
    node_grad_ref[...] = full2[...]
    for d in range(PL):
        q = lax.rem(p + PL - d, PL)
        for e in range(1, C):
            i = d * (C - 1) + e - 1
            there = lax.rem(r + C - e, C) * rows_w + q * w1
            arrived(gw_rows(there, w1), rg_s.at[i], rg_r.at[i], r_peer(e))
    gw_ref[...] = gw[...]
    for c in sends:
        c.wait_send()
    z_drain(nodes, x, x_s, x_r)
    z_drain(gs, x2, x2_s, x2_r)


def shards(Z, PL, C, nodes, adjacency, gain, w_in, w_out, cotangent):
    group, D = nodes.shape
    ppr = Z // C
    pc = group // C
    rows_w = 2 * D // C
    w1 = rows_w // PL
    spread = w1 % (16 * Z) == 0
    wz = w1 // Z if spread else w1
    V = pltpu.VMEM
    S = pltpu.SemaphoreType.DMA

    def pair(n):
        return [S((n,)), S((n,))]

    scratch = [
        V((group, D), BF16), V((D, D), BF16), V((D, D), BF16), V((group, D), BF16),
        V((PL * group, ppr * group), BF16), V((ppr * group, D), BF16), V((ppr * group, D), BF16),
        V((C, PL, pc, D), F32), V((C - 1, PL, pc, D), F32), V((PL - 1, pc, D), F32),
        V((PL - 1, pc, D), F32), V((group, D), F32),
        V((C, PL, pc, D), BF16), V((C - 1, PL, pc, D), BF16), V((PL - 1, pc, D), BF16),
        V((PL - 1, pc, D), BF16), V((group, D), BF16),
        V((group, D), BF16), V((2, group, D), BF16), V((2, group, D), BF16),
        V((PL, w1, D), BF16), V((PL - 1, w1, D), BF16),
        V((Z if spread else 1, wz, D), BF16), V((Z - 1 if spread else Z, wz, D), BF16),
        V((2 * D, D), BF16),
        V((8, D), F32), V((PL, 8, D), F32), V((Z, 8, D), F32),
        S((4 + ppr,)),
        *pair((PL - 1) * ppr),
        S((Z - 1,)), S((ppr,)), S((Z - 1,)), S((ppr,)),
        *pair(C - 1), *pair(PL - 1), *pair(C - 1),
        *pair(C - 1), *pair(PL - 1), *pair(C - 1),
        *pair(PL - 1), *pair(Z - 1), *pair(Z - 1), *pair(PL - 1), *pair(PL * (C - 1)),
        *pair(PL - 1), *pair(Z - 1),
    ]
    A = pl.BlockSpec(memory_space=pl.ANY)
    M = pl.BlockSpec(memory_space=pltpu.VMEM)
    node_out, node_grad, gw, gg = pl.pallas_call(
        functools.partial(kernel, Z, PL, C, spread),
        out_shape=[
            jax.ShapeDtypeStruct((group, D), BF16),
            jax.ShapeDtypeStruct((group, D), BF16),
            jax.ShapeDtypeStruct((2 * D, D), BF16),
            jax.ShapeDtypeStruct((8, D), F32),
        ],
        in_specs=[A, A, M, A, A, A],
        out_specs=[M, M, M, M],
        scratch_shapes=scratch,
        compiler_params=pltpu.CompilerParams(
            collective_id=0, has_side_effects=True, vmem_limit_bytes=40 * 1024 * 1024
        ),
    )(nodes, adjacency, gain.reshape(1, D), w_in, w_out, cotangent)
    gw = gw.astype(F32)
    return node_out, node_grad, gw[:D], gw[D:], gg[0]


def solution(mesh):
    R, C = mesh.shape["rows"], mesh.shape["rep"]
    PL = math.isqrt(R)
    return jax.shard_map(
        functools.partial(shards, R // PL, PL, C),
        mesh=mesh,
        in_specs=(P("rows", None), P("rows", "rep"), P(), P(), P(), P("rows", None)),
        out_specs=(P("rows", None), P("rows", None), P(), P(), P()),
        check_vma=False,
    )
```

time: 449 us -> 58.1 us (0.13)
  waiting for transfers between devices: 371 us -> 0 us
  Pallas kernels: 0 us -> 48.1 us
  blocking collectives: 33.3 us -> 0 us
  between operations: 14.1 us -> 0.66 us
  matrix products: 10.9 us -> 0 us
  local copies, waits for them, and re-layouts: 14.5 us -> 9 us
  other arithmetic: 4.78 us -> 0 us
    psum x5 -> x0, waiting for transfers between devices: 371 us -> none  [the longest x2 239 us: broadcast(): return lax.psum(jnp.where(mine, x, jnp.zeros_like(x)), axis)]
    pallas_call x0 -> x1, Pallas kernels: none -> 48.1 us  [shards(): pl.pallas_call(functools.partial(kernel, Z, PL, C, spread), out_shape=[ja...]
    psum x1 -> x0, blocking collectives: 33.3 us -> none  [shards(): lax.psum((grad_w_in, grad_w_out, grad_gain), 'rows')]
    dot_general x22 -> x0, matrix products: 10.9 us -> none  [the longest x16 6.33 us: aggregate(): jnp.dot(columns, owner_block, preferred_element_type=jnp.float32)]
    unnamed x49 -> x14, local copies, waits for them, and re-layouts: 14.5 us -> 6.82 us
  transfers between devices with their start and end apart: 5 -> 0, of which waited for: 4 -> 0; matrix products, arithmetic and copies ran while one was open for 1% -> 0% of each run, Pallas kernels for 0% -> 0%
where the time goes in v1:
time: 58.1 us; the launch traced here: 57.8 us
  Pallas kernels  48.1 us (83%)
  local copies, waits for them, and re-layouts  9 us (15%)
  between operations  0.66 us (1%)
    pallas_call x1, Pallas kernels, shards(): pl.pallas_call(functools.partial(kernel, Z, PL, C, spread), out_shape=[ja...  48.1 us
    unnamed x14, local copies, waits for them, and re-layouts  6.82 us
    slice x2, local copies, waits for them, and re-layouts, shards(): return (node_out, node_grad, gw[:D], gw[D:], gg[0])  2.18 us

profile of v1, /device:TPU:1, one launch (start us, length us, event | category | flops | bytes accessed | tf_op | source)
XLA Modules:
  0.0 57.8 jit_solution(9575252757920358791)
XLA Ops:
  0.6 0.0 copy-start
  0.6 1.0 %copy-done = bf16[512,512]{1,0:T(8,128)(2,1)S(1)} copy-done((bf16[512,512]{1,0:T(8,128)(2,1)S(1)}, bf16[512,512]{1,0:T(8,128)(2,1)}, u32[]{:S(2)}) %copy-start) | copy-done | bytes 524312
  1.7 0.0 copy-start.1
  1.7 1.0 %copy-done.1 = bf16[512,512]{1,0:T(8,128)(2,1)S(1)} copy-done((bf16[512,512]{1,0:T(8,128)(2,1)S(1)}, bf16[512,512]{1,0:T(8,128)(2,1)}, u32[]{:S(2)}) %copy-start.1) | copy-done | bytes 524312
  2.7 0.0 copy-start.2
  2.7 0.9 %copy-done.2 = bf16[128,1024]{1,0:T(8,128)(2,1)S(1)} copy-done((bf16[128,1024]{1,0:T(8,128)(2,1)S(1)}, bf16[128,1024]{1,0:T(8,128)(2,1)}, u32[]{:S(2)}) %copy-start.2) | copy-done | bytes 262168
  3.7 0.0 copy-start.3
  3.7 0.9 %copy-done.3 = bf16[128,512]{1,0:T(8,128)(2,1)S(1)} copy-done((bf16[128,512]{1,0:T(8,128)(2,1)S(1)}, bf16[128,512]{1,0:T(8,128)(2,1)}, u32[]{:S(2)}) %copy-start.3) | copy-done | bytes 131096
  4.6 0.0 copy-start.4
  4.6 0.9 %copy-done.4 = bf16[128,512]{1,0:T(8,128)(2,1)S(1)} copy-done((bf16[128,512]{1,0:T(8,128)(2,1)S(1)}, bf16[128,512]{1,0:T(8,128)(2,1)}, u32[]{:S(2)}) %copy-start.4) | copy-done | bytes 131096
  5.5 0.0 copy-start.5
  5.5 0.7 %copy-done.5 = f32[512]{0:T(512)S(1)} copy-done((f32[512]{0:T(512)S(1)}, f32[512]{0:T(512)}, u32[]{:S(2)}) %copy-start.5) | copy-done | bytes 2072
  6.2 48.1 %shard_map.101 = (bf16[128,512]{1,0:T(8,128)(2,1)S(1)}, bf16[128,512]{1,0:T(8,128)(2,1)S(1)}, bf16[1024,512]{1,0:T(8,128)(2,1)S(1)}, f32[8,512]{1,0:T(8,128)S(1)}) custom-call(bf16[128,512]{1,0:T(8,128)(2,1)S(1)} %copy-done.3, bf16[128,1024]{1,0:T(8,128)(2,1)S(1)} %copy-done.2, f32[1,512]{1,0:T(1,128)S(1)} %bitcast.2, bf16[512,512]{1,0:T(8,128)(2,1)S(1)} %copy-done, ...), custom_call_target="tpu_custom_call" | custom-call | tf_op jit(solution)/shard_map/pallas_call | solution.py:348
  54.3 0.6 %slice.11 = f32[1,512]{1,0:T(1,128)} slice(f32[8,512]{1,0:T(8,128)S(1)} %get-tuple-element.12), slice={[0:1], [0:512]} | slice | bytes 4096 | tf_op jit(solution)/shard_map/slice | solution.py:364
  54.9 1.6 %fusion = (f32[512,512]{1,0:T(8,128)}, f32[512,512]{1,0:T(8,128)}) fusion(bf16[1024,512]{1,0:T(8,128)(2,1)S(1)} %get-tuple-element.11), kind=kLoop, calls=%fused_computation | loop fusion | bytes 4194304 | tf_op jit(solution)/shard_map/slice | solution.py:364
  56.5 0.7 %copy.13 = bf16[128,512]{1,0:T(8,128)(2,1)} copy(bf16[128,512]{1,0:T(8,128)(2,1)S(1)} %get-tuple-element.20) | data formatting | bytes 262144
  57.1 0.7 %copy.14 = bf16[128,512]{1,0:T(8,128)(2,1)} copy(bf16[128,512]{1,0:T(8,128)(2,1)S(1)} %get-tuple-element.21) | data formatting | bytes 262144
Async XLA Ops:
  0.6 1.0 %copy-start = (bf16[512,512]{1,0:T(8,128)(2,1)S(1)}, bf16[512,512]{1,0:T(8,128)(2,1)}, u32[]{:S(2)}) copy-start(bf16[512,512]{1,0:T(8,128)(2,1)} %w_in_h.1) | copy-start | bytes 1572868
  1.7 1.0 %copy-start.1 = (bf16[512,512]{1,0:T(8,128)(2,1)S(1)}, bf16[512,512]{1,0:T(8,128)(2,1)}, u32[]{:S(2)}) copy-start(bf16[512,512]{1,0:T(8,128)(2,1)} %w_out_h.1) | copy-start | bytes 1572868
  2.7 0.9 %copy-start.2 = (bf16[128,1024]{1,0:T(8,128)(2,1)S(1)}, bf16[128,1024]{1,0:T(8,128)(2,1)}, u32[]{:S(2)}) copy-start(bf16[128,1024]{1,0:T(8,128)(2,1)} %adj_h.1) | copy-start | bytes 786436
  3.7 0.9 %copy-start.3 = (bf16[128,512]{1,0:T(8,128)(2,1)S(1)}, bf16[128,512]{1,0:T(8,128)(2,1)}, u32[]{:S(2)}) copy-start(bf16[128,512]{1,0:T(8,128)(2,1)} %nodes_h.1) | copy-start | bytes 393220
  4.6 0.9 %copy-start.4 = (bf16[128,512]{1,0:T(8,128)(2,1)S(1)}, bf16[128,512]{1,0:T(8,128)(2,1)}, u32[]{:S(2)}) copy-start(bf16[128,512]{1,0:T(8,128)(2,1)} %cot_h.1) | copy-start | bytes 393220
  5.5 0.7 %copy-start.5 = (f32[512]{0:T(512)S(1)}, f32[512]{0:T(512)}, u32[]{:S(2)}) copy-start(f32[512]{0:T(512)} %param.8) | copy-start | bytes 6148

commit v2 on v1

--- a/solution.py
+++ b/solution.py
@@ -20,11 +20,11 @@
 def kernel(
     Z, PL, C, spread,
     nodes_h, adj_h, gain_ref, w_in_h, w_out_h, cot_h,
-    node_out_ref, node_grad_ref, gw_ref, gg_ref,
+    node_out_h, node_grad_h, gw_h, gg_h,
     nodes, w_in, w_out, cot, a2, x, x2,
     part, cin, acc, pin, full, part2, cin2, acc2, pin2, full2,
-    gs, lh, rh, gpart, gin, gz, gzin, gw, gg, ggp, ggz,
-    loc, a_s, a_r, x_s, x_r, x2_s, x2_r,
+    gs, lh, rh, gpart, gin, gz, gzin, gw, gg, ggp, ggz, no_v, gg_v,
+    loc, st, a_s, a_r, x_s, x_r, x2_s, x2_r,
     c_s, c_r, p_s, p_r, f_s, f_r, c2_s, c2_r, p2_s, p2_r, f2_s, f2_r,
     g_s, g_r, z_s, z_r, zg_s, zg_r, pg_s, pg_r, rg_s, rg_r,
     ggp_s, ggp_r, ggz_s, ggz_r,
@@ -40,6 +40,12 @@
     zl = lax.rem(z, ppr)
     owner = lax.div(z, ppr) == r
     sends = []
+    stores = []
+
+    def store(src, dst):
+        c = pltpu.make_async_copy(src, dst, st.at[len(stores)])
+        c.start()
+        stores.append(c)
 
     def z_peer(d):
         return {"rows": lax.rem(z + d, Z) * PL + p}
@@ -137,22 +143,25 @@
                 a_s.at[(d - 1) * ppr + k], a_r.at[(d - 1) * ppr + k], p_peer(d),
             )
 
+    order = list(range(1, PL)) + [0]
+
     def partials(buf, out, ins, ss, rs):
-        for q in range(PL):
-            val = dot(a2[q * group:(q + 1) * group], buf[...])
+        for d in order:
+            q = lax.rem(p + d, PL)
+            val = dot(a2[pl.ds(pl.multiple_of(q * group, group), group)], buf[...])
             for c in range(C):
-                out[c, q] = val[c * pc:(c + 1) * pc].astype(out.dtype)
-        for d in range(1, C):
-            send(out.at[lax.rem(r + d, C)], ins.at[d - 1], ss.at[d - 1], rs.at[d - 1], r_peer(d))
+                out[c, d] = val[c * pc:(c + 1) * pc].astype(out.dtype)
+            for e in range(1, C):
+                i = d * (C - 1) + e - 1
+                send(out.at[lax.rem(r + e, C), d], ins.at[e - 1, d], ss.at[i], rs.at[i], r_peer(e))
 
     def combine(out, ins, ss, rs, accs, pins, pss, prs):
-        for d in range(1, C):
-            arrived(ins.at[d - 1], ss.at[d - 1], rs.at[d - 1], r_peer(d))
-        for d in list(range(1, PL)) + [0]:
-            q = lax.rem(p + d, PL)
-            val = out[r, q].astype(F32)
-            for e in range(C - 1):
-                val = val + ins[e, q].astype(F32)
+        for d in order:
+            val = out[r, d].astype(F32)
+            for e in range(1, C):
+                i = d * (C - 1) + e - 1
+                arrived(ins.at[e - 1, d], ss.at[i], rs.at[i], r_peer(e))
+                val = val + ins[e - 1, d].astype(F32)
             if d == 0:
                 return val
             accs[d - 1] = val.astype(accs.dtype)
@@ -216,7 +225,8 @@
     ggp[p] = gg[...]
     for d in range(1, PL):
         send(gg, ggp.at[p], ggp_s.at[d - 1], ggp_r.at[d - 1], p_peer(d))
-    node_out_ref[...] = (nodes[...].astype(F32) + dot(hidden, w_out[...])).astype(BF16)
+    no_v[...] = (nodes[...].astype(F32) + dot(hidden, w_out[...])).astype(BF16)
+    store(no_v, node_out_h)
 
     z_wait(gs, x2, x2_s, x2_r)
     partials(x2, part2, cin2, c2_s, c2_r)
@@ -226,8 +236,9 @@
         arrived(gin.at[d - 1], g_s.at[d - 1], g_r.at[d - 1], p_peer(d))
         gsum = gsum + gin[d - 1].astype(F32)
     base = r * rows_w + p * w1
+    wz = w1 // Z if spread else w1
+    nz = Z if spread else 1
     if spread:
-        wz = w1 // Z
         for k in range(Z):
             gz[k] = gsum[k * wz:(k + 1) * wz].astype(BF16)
         for d in range(1, Z):
@@ -269,44 +280,84 @@
             shard = shard + gzin[k].astype(F32)
         gw[pl.ds(pl.multiple_of(base, w1), w1)] = shard.astype(BF16)
 
+    def plane_send(start, count, k):
+        for d in range(1, PL):
+            i = k * (PL - 1) + d - 1
+            send(gw_rows(start, count), gw_rows(start, count), pg_s.at[i], pg_r.at[i], p_peer(d))
+
+    plane_send(base + z * wz if spread else base, wz, 0)
+
     back = finish(own2, acc2, pin2, p2_s, p2_r)
     full2[mine] = (cot[mine].astype(F32) + back).astype(BF16)
     share(full2, f2_s, f2_r)
 
-    if spread:
-        for d in range(1, Z):
-            there = base + lax.rem(z + Z - d, Z) * wz
-            arrived(gw_rows(there, wz), zg_s.at[d - 1], zg_r.at[d - 1], z_peer(d))
-    for d in range(1, PL):
-        send(gw_rows(base, w1), gw_rows(base, w1), pg_s.at[d - 1], pg_r.at[d - 1], p_peer(d))
+    for k in range(1, nz):
+        there = base + lax.rem(z + Z - k, Z) * wz
+        arrived(gw_rows(there, wz), zg_s.at[k - 1], zg_r.at[k - 1], z_peer(k))
+        plane_send(there, wz, k)
     for d in range(PL):
         q = lax.rem(p + PL - d, PL)
-        block = gw_rows(r * rows_w + q * w1, w1)
+        start = r * rows_w + q * w1
         if d > 0:
-            arrived(block, pg_s.at[d - 1], pg_r.at[d - 1], p_peer(d))
+            for k in range(nz):
+                there = start + lax.rem(z + Z - k, Z) * wz if spread else start
+                i = k * (PL - 1) + d - 1
+                arrived(gw_rows(there, wz), pg_s.at[i], pg_r.at[i], p_peer(d))
+        block = gw_rows(start, w1)
         for e in range(1, C):
             i = d * (C - 1) + e - 1
             send(block, block, rg_s.at[i], rg_r.at[i], r_peer(e))
+        store(block, gw_h.at[pl.ds(pl.multiple_of(start, w1), w1)])
 
     for d in range(1, Z):
         arrived(ggz.at[lax.rem(z + Z - d, Z)], ggz_s.at[d - 1], ggz_r.at[d - 1], z_peer(d))
     ggv = ggz[0]
     for k in range(1, Z):
         ggv = ggv + ggz[k]
-    gg_ref[...] = ggv
+    gg_v[...] = ggv[:1]
+    store(gg_v, gg_h)
     shared(full2, f2_s, f2_r)
-    node_grad_ref[...] = full2[...]
+    store(full2, node_grad_h)
     for d in range(PL):
         q = lax.rem(p + PL - d, PL)
         for e in range(1, C):
             i = d * (C - 1) + e - 1
             there = lax.rem(r + C - e, C) * rows_w + q * w1
             arrived(gw_rows(there, w1), rg_s.at[i], rg_r.at[i], r_peer(e))
-    gw_ref[...] = gw[...]
+            store(gw_rows(there, w1), gw_h.at[pl.ds(pl.multiple_of(there, w1), w1)])
     for c in sends:
         c.wait_send()
     z_drain(nodes, x, x_s, x_r)
     z_drain(gs, x2, x2_s, x2_r)
+    for c in stores:
+        c.wait()
+
+
+def closing(
+    chunks, node_out, node_grad, gw, gg, o_out, o_grad, o_win, o_wout, o_gain,
+    narrow, wide, pair, gain, sem_in, sem_out,
+):
+    D = o_win.shape[0]
+    rows = 2 * D // chunks
+    cuts = [pl.ds(k * rows, rows) for k in range(chunks)]
+    steps = [(gw.at[c], narrow.at[c]) for c in cuts]
+    steps += [(node_out, pair.at[0]), (node_grad, pair.at[1]), (gg, gain)]
+    loads = [pltpu.make_async_copy(a, b, sem_in.at[i]) for i, (a, b) in enumerate(steps)]
+    for c in loads:
+        c.start()
+    outs = []
+    for k in range(chunks):
+        loads[k].wait()
+        wide[cuts[k]] = narrow[cuts[k]].astype(F32)
+        dst = o_win if k * rows < D else o_wout
+        outs.append((wide.at[cuts[k]], dst.at[pl.ds(k * rows % D, rows)]))
+        pltpu.make_async_copy(*outs[k], sem_out.at[k]).start()
+    outs += [(pair.at[0], o_out), (pair.at[1], o_grad), (gain, o_gain)]
+    for k in range(chunks, chunks + 3):
+        loads[k].wait()
+        pltpu.make_async_copy(*outs[k], sem_out.at[k]).start()
+    for k in range(chunks + 3):
+        pltpu.make_async_copy(*outs[k], sem_out.at[k]).wait()
 
 
 def shards(Z, PL, C, nodes, adjacency, gain, w_in, w_out, cotangent):
@@ -334,34 +385,51 @@
         V((PL, w1, D), BF16), V((PL - 1, w1, D), BF16),
         V((Z if spread else 1, wz, D), BF16), V((Z - 1 if spread else Z, wz, D), BF16),
         V((2 * D, D), BF16),
-        V((8, D), F32), V((PL, 8, D), F32), V((Z, 8, D), F32),
-        S((4 + ppr,)),
+        V((8, D), F32), V((PL, 8, D), F32), V((Z, 8, D), F32), V((group, D), BF16), V((1, D), F32),
+        S((4 + ppr,)), S((3 + PL * C,)),
         *pair((PL - 1) * ppr),
         S((Z - 1,)), S((ppr,)), S((Z - 1,)), S((ppr,)),
-        *pair(C - 1), *pair(PL - 1), *pair(C - 1),
-        *pair(C - 1), *pair(PL - 1), *pair(C - 1),
-        *pair(PL - 1), *pair(Z - 1), *pair(Z - 1), *pair(PL - 1), *pair(PL * (C - 1)),
+        *pair(PL * (C - 1)), *pair(PL - 1), *pair(C - 1),
+        *pair(PL * (C - 1)), *pair(PL - 1), *pair(C - 1),
+        *pair(PL - 1), *pair(Z - 1), *pair(Z - 1), *pair((PL - 1) * (w1 // wz)), *pair(PL * (C - 1)),
         *pair(PL - 1), *pair(Z - 1),
     ]
-    A = pl.BlockSpec(memory_space=pl.ANY)
+    H = pl.BlockSpec(memory_space=pltpu.HBM)
     M = pl.BlockSpec(memory_space=pltpu.VMEM)
-    node_out, node_grad, gw, gg = pl.pallas_call(
+    parts = pl.pallas_call(
         functools.partial(kernel, Z, PL, C, spread),
         out_shape=[
             jax.ShapeDtypeStruct((group, D), BF16),
             jax.ShapeDtypeStruct((group, D), BF16),
             jax.ShapeDtypeStruct((2 * D, D), BF16),
-            jax.ShapeDtypeStruct((8, D), F32),
+            jax.ShapeDtypeStruct((1, D), F32),
         ],
-        in_specs=[A, A, M, A, A, A],
-        out_specs=[M, M, M, M],
+        in_specs=[H, H, M, H, H, H],
+        out_specs=[H, H, H, H],
         scratch_shapes=scratch,
         compiler_params=pltpu.CompilerParams(
-            collective_id=0, has_side_effects=True, vmem_limit_bytes=40 * 1024 * 1024
+            collective_id=0, has_side_effects=True, vmem_limit_bytes=60 * 1024 * 1024
         ),
     )(nodes, adjacency, gain.reshape(1, D), w_in, w_out, cotangent)
-    gw = gw.astype(F32)
-    return node_out, node_grad, gw[:D], gw[D:], gg[0]
+    chunks = 8
+    node_out, node_grad, g_in, g_out, gg = pl.pallas_call(
+        functools.partial(closing, chunks),
+        out_shape=[
+            jax.ShapeDtypeStruct((group, D), BF16),
+            jax.ShapeDtypeStruct((group, D), BF16),
+            jax.ShapeDtypeStruct((D, D), F32),
+            jax.ShapeDtypeStruct((D, D), F32),
+            jax.ShapeDtypeStruct((1, D), F32),
+        ],
+        in_specs=[H, H, H, H],
+        out_specs=[H, H, H, H, H],
+        scratch_shapes=[
+            V((2 * D, D), BF16), V((2 * D, D), F32), V((2, group, D), BF16), V((1, D), F32),
+            S((chunks + 3,)), S((chunks + 3,)),
+        ],
+        compiler_params=pltpu.CompilerParams(vmem_limit_bytes=60 * 1024 * 1024),
+    )(*parts)
+    return node_out, node_grad, g_in, g_out, gg.reshape(D)
 
 
 def solution(mesh):

time: 58.1 us -> 53 us (0.912)
  local copies, waits for them, and re-layouts: 9 us -> 0 us
  Pallas kernels: 48.1 us -> 52.2 us
    unnamed x14 -> x0, local copies, waits for them, and re-layouts: 6.82 us -> none
    pallas_call x0 -> x1, Pallas kernels: none -> 2.51 us  [shards(): pl.pallas_call(functools.partial(closing, chunks), out_shape=[jax.ShapeDt...]
    slice x2 -> x0, local copies, waits for them, and re-layouts: 2.18 us -> none  [shards(): return (node_out, node_grad, gw[:D], gw[D:], gg[0])]
    pallas_call x1, Pallas kernels: 48.1 us -> 49.7 us  [shards(): pl.pallas_call(functools.partial(kernel, Z, PL, C, spread), out_shape=[ja...]
where the time goes in v2:
time: 53 us; the launch traced here: 52.8 us
  Pallas kernels  52.2 us (98%)
  between operations  0.64 us (1%)
    pallas_call x1, Pallas kernels, shards(): pl.pallas_call(functools.partial(kernel, Z, PL, C, spread), out_shape=[ja...  49.7 us
    pallas_call x1, Pallas kernels, shards(): pl.pallas_call(functools.partial(closing, chunks), out_shape=[jax.ShapeDt...  2.51 us

profile of v2, /device:TPU:1, one launch (start us, length us, event | category | flops | bytes accessed | tf_op | source)
XLA Modules:
  0.0 52.8 jit_solution(12242629959617957911)
XLA Ops:
  0.6 49.7 %shard_map.101 = (bf16[128,512]{1,0:T(8,128)(2,1)}, bf16[128,512]{1,0:T(8,128)(2,1)}, bf16[1024,512]{1,0:T(8,128)(2,1)}, f32[1,512]{1,0:T(1,128)}) custom-call(bf16[128,512]{1,0:T(8,128)(2,1)} %nodes_h.1, bf16[128,1024]{1,0:T(8,128)(2,1)} %adj_h.1, f32[1,512]{1,0:T(1,128)} %bitcast.2, bf16[512,512]{1,0:T(8,128)(2,1)} %w_in_h.1, bf16[512,512]{1,0:T(8,128)(2,1)} %w_out_h.1, ...), custom_call_target="tpu_custom_call" | custom-call | tf_op jit(solution)/shard_map/pallas_call | solution.py:399
  50.3 2.5 %shard_map.102 = (bf16[128,512]{1,0:T(8,128)(2,1)}, bf16[128,512]{1,0:T(8,128)(2,1)}, f32[512,512]{1,0:T(8,128)}, f32[512,512]{1,0:T(8,128)}, f32[1,512]{1,0:T(1,128)}) custom-call(bf16[128,512]{1,0:T(8,128)(2,1)} %get-tuple-element.14.node_out, bf16[128,512]{1,0:T(8,128)(2,1)} %get-tuple-element.15.node_grad, bf16[1024,512]{1,0:T(8,128)(2,1)} %get-tuple-element.16.gw, ...), custom_call_target="tpu_custom_call" | custom-call | tf_op jit(solution)/shard_map/pallas_call | solution.py:415

commit v3 on v2

--- a/solution.py
+++ b/solution.py
@@ -18,7 +18,7 @@
 
 
 def kernel(
-    Z, PL, C, spread,
+    Z, PL, C, T, spread,
     nodes_h, adj_h, gain_ref, w_in_h, w_out_h, cot_h,
     node_out_h, node_grad_h, gw_h, gg_h,
     nodes, w_in, w_out, cot, a2, x, x2,
@@ -35,8 +35,9 @@
     ppr = Z // C
     group, D = nodes.shape
     pc = group // C
-    rows_w = 2 * D // C
+    rows_w = 2 * D // C // T
     w1 = rows_w // PL
+    wz = w1 // Z if spread else w1
     zl = lax.rem(z, ppr)
     owner = lax.div(z, ppr) == r
     sends = []
@@ -200,6 +201,26 @@
     pre = dot(lifted, w_in[...])
     sigma = jax.nn.sigmoid(pre)
     hidden = (pre * sigma).astype(BF16)
+
+    def first_row(t, rep):
+        if T == 1:
+            return rep * rows_w
+        return (1 - t) * D + rep * rows_w
+
+    def weights_start(t, left, right):
+        gval = dot(left, right, 0, 0)
+        for q in range(PL):
+            gpart[t, q] = gval[q * w1:(q + 1) * w1].astype(BF16)
+        for d in range(1, PL):
+            i = t * (PL - 1) + d - 1
+            send(gpart.at[t, lax.rem(p + d, PL)], gin.at[i], g_s.at[i], g_r.at[i], p_peer(d))
+
+    def columns(ref):
+        return ref[:, pl.ds(pl.multiple_of(r * rows_w, rows_w), rows_w)]
+
+    lh[1] = hidden
+    if T == 2:
+        weights_start(0, columns(lh.at[1]), cot[...])
     grad_pre = (grad_hidden * sigma * (1.0 + pre * (1.0 - sigma))).astype(BF16)
     grad_lifted = dot(grad_pre, w_in[...], 1, 1)
     grad_normed = grad_lifted * gain
@@ -209,18 +230,15 @@
     z_start(gs, x2, x2_s, x2_r)
 
     lh[0] = lifted
-    lh[1] = hidden
-    rh[0] = grad_pre
-    rh[1] = cot[...]
-    half = C // 2
-    which = lax.div(r, half)
-    first = lax.rem(r, half) * rows_w
-    left = lh[which, :, pl.ds(pl.multiple_of(first, rows_w), rows_w)] if half > 1 else lh[which]
-    gval = dot(left, rh[which], 0, 0)
-    for q in range(PL):
-        gpart[q] = gval[q * w1:(q + 1) * w1].astype(BF16)
-    for d in range(1, PL):
-        send(gpart.at[lax.rem(p + d, PL)], gin.at[d - 1], g_s.at[d - 1], g_r.at[d - 1], p_peer(d))
+    if T == 2:
+        weights_start(1, columns(lh.at[0]), grad_pre)
+    else:
+        rh[0] = grad_pre
+        rh[1] = cot[...]
+        half = C // 2
+        which = lax.div(r, half)
+        here = pl.multiple_of(lax.rem(r, half) * rows_w, rows_w)
+        weights_start(0, lh[which, :, pl.ds(here, rows_w)], rh[which])
     gg[...] = jnp.broadcast_to(jnp.sum(grad_lifted * normed, axis=0, keepdims=True), gg.shape)
     ggp[p] = gg[...]
     for d in range(1, PL):
@@ -228,26 +246,93 @@
     no_v[...] = (nodes[...].astype(F32) + dot(hidden, w_out[...])).astype(BF16)
     store(no_v, node_out_h)
 
+    def gw_rows(start, count):
+        return gw.at[pl.ds(pl.multiple_of(start, count), count)]
+
+    def scatter_z(t):
+        gsum = gpart[t, p].astype(F32)
+        for d in range(1, PL):
+            i = t * (PL - 1) + d - 1
+            arrived(gin.at[i], g_s.at[i], g_r.at[i], p_peer(d))
+            gsum = gsum + gin[i].astype(F32)
+        if spread:
+            for k in range(Z):
+                gz[t, k] = gsum[k * wz:(k + 1) * wz].astype(BF16)
+        else:
+            gz[t, 0] = gsum.astype(BF16)
+            gzin[t, z] = gz[t, 0]
+        for d in range(1, Z):
+            i = t * (Z - 1) + d - 1
+            src = gz.at[t, lax.rem(z + d, Z)] if spread else gz.at[t, 0]
+            dst = gzin.at[t, d - 1] if spread else gzin.at[t, z]
+            send(src, dst, z_s.at[i], z_r.at[i], z_peer(d))
+
+    def gather_z(t):
+        base = first_row(t, r) + p * w1
+        shard = gz[t, z].astype(F32) if spread else None
+        for d in range(1, Z):
+            i = t * (Z - 1) + d - 1
+            slot = gzin.at[t, d - 1] if spread else gzin.at[t, lax.rem(z + Z - d, Z)]
+            arrived(slot, z_s.at[i], z_r.at[i], z_peer(d))
+            if spread:
+                shard = shard + gzin[t, d - 1].astype(F32)
+        if not spread:
+            shard = gzin[t, 0].astype(F32)
+            for k in range(1, Z):
+                shard = shard + gzin[t, k].astype(F32)
+            gw[pl.ds(pl.multiple_of(base, w1), w1)] = shard.astype(BF16)
+            return
+        here = base + z * wz
+        gw[pl.ds(pl.multiple_of(here, wz), wz)] = shard.astype(BF16)
+        for d in range(1, Z):
+            i = t * (Z - 1) + d - 1
+            send(gw_rows(here, wz), gw_rows(here, wz), zg_s.at[i], zg_r.at[i], z_peer(d))
+
+    def gather_plane(t):
+        base = first_row(t, r) + p * w1
+        if spread:
+            for d in range(1, Z):
+                i = t * (Z - 1) + d - 1
+                there = base + lax.rem(z + Z - d, Z) * wz
+                arrived(gw_rows(there, wz), zg_s.at[i], zg_r.at[i], z_peer(d))
+        for d in range(1, PL):
+            i = t * (PL - 1) + d - 1
+            send(gw_rows(base, w1), gw_rows(base, w1), pg_s.at[i], pg_r.at[i], p_peer(d))
+
+    def keep(start):
+        store(gw_rows(start, w1), gw_h.at[pl.ds(pl.multiple_of(start, w1), w1)])
+
+    def gather_rep(t):
+        for d in range(PL):
+            start = first_row(t, r) + lax.rem(p + PL - d, PL) * w1
+            block = gw_rows(start, w1)
+            if d > 0:
+                i = t * (PL - 1) + d - 1
+                arrived(block, pg_s.at[i], pg_r.at[i], p_peer(d))
+            for e in range(1, C):
+                i = (t * PL + d) * (C - 1) + e - 1
+                send(block, block, rg_s.at[i], rg_r.at[i], r_peer(e))
+            keep(start)
+
+    def gather_end(t):
+        for d in range(PL):
+            for e in range(1, C):
+                i = (t * PL + d) * (C - 1) + e - 1
+                start = first_row(t, lax.rem(r + C - e, C)) + lax.rem(p + PL - d, PL) * w1
+                arrived(gw_rows(start, w1), rg_s.at[i], rg_r.at[i], r_peer(e))
+                keep(start)
+
+    last = T - 1
+    for t in range(T):
+        scatter_z(t)
+    if T == 2:
+        gather_z(0)
     z_wait(gs, x2, x2_s, x2_r)
     partials(x2, part2, cin2, c2_s, c2_r)
-
-    gsum = gpart[p].astype(F32)
-    for d in range(1, PL):
-        arrived(gin.at[d - 1], g_s.at[d - 1], g_r.at[d - 1], p_peer(d))
-        gsum = gsum + gin[d - 1].astype(F32)
-    base = r * rows_w + p * w1
-    wz = w1 // Z if spread else w1
-    nz = Z if spread else 1
-    if spread:
-        for k in range(Z):
-            gz[k] = gsum[k * wz:(k + 1) * wz].astype(BF16)
-        for d in range(1, Z):
-            send(gz.at[lax.rem(z + d, Z)], gzin.at[d - 1], z_s.at[d - 1], z_r.at[d - 1], z_peer(d))
-    else:
-        gz[0] = gsum.astype(BF16)
-        gzin[z] = gz[0]
-        for d in range(1, Z):
-            send(gz.at[0], gzin.at[z], z_s.at[d - 1], z_r.at[d - 1], z_peer(d))
+    gather_z(last)
+    own2 = combine(part2, cin2, c2_s, c2_r, acc2, pin2, p2_s, p2_r)
+    for t in range(T):
+        gather_plane(t)
 
     for d in range(1, PL):
         arrived(ggp.at[lax.rem(p + PL - d, PL)], ggp_s.at[d - 1], ggp_r.at[d - 1], p_peer(d))
@@ -258,57 +343,14 @@
     for d in range(1, Z):
         send(ggz.at[z], ggz.at[z], ggz_s.at[d - 1], ggz_r.at[d - 1], z_peer(d))
 
-    own2 = combine(part2, cin2, c2_s, c2_r, acc2, pin2, p2_s, p2_r)
-
-    def gw_rows(start, count):
-        return gw.at[pl.ds(pl.multiple_of(start, count), count)]
-
-    if spread:
-        shard = gz[z].astype(F32)
-        for d in range(1, Z):
-            arrived(gzin.at[d - 1], z_s.at[d - 1], z_r.at[d - 1], z_peer(d))
-            shard = shard + gzin[d - 1].astype(F32)
-        here = base + z * wz
-        gw[pl.ds(pl.multiple_of(here, wz), wz)] = shard.astype(BF16)
-        for d in range(1, Z):
-            send(gw_rows(here, wz), gw_rows(here, wz), zg_s.at[d - 1], zg_r.at[d - 1], z_peer(d))
-    else:
-        for d in range(1, Z):
-            arrived(gzin.at[lax.rem(z + Z - d, Z)], z_s.at[d - 1], z_r.at[d - 1], z_peer(d))
-        shard = gzin[0].astype(F32)
-        for k in range(1, Z):
-            shard = shard + gzin[k].astype(F32)
-        gw[pl.ds(pl.multiple_of(base, w1), w1)] = shard.astype(BF16)
-
-    def plane_send(start, count, k):
-        for d in range(1, PL):
-            i = k * (PL - 1) + d - 1
-            send(gw_rows(start, count), gw_rows(start, count), pg_s.at[i], pg_r.at[i], p_peer(d))
-
-    plane_send(base + z * wz if spread else base, wz, 0)
-
     back = finish(own2, acc2, pin2, p2_s, p2_r)
     full2[mine] = (cot[mine].astype(F32) + back).astype(BF16)
     share(full2, f2_s, f2_r)
-
-    for k in range(1, nz):
-        there = base + lax.rem(z + Z - k, Z) * wz
-        arrived(gw_rows(there, wz), zg_s.at[k - 1], zg_r.at[k - 1], z_peer(k))
-        plane_send(there, wz, k)
-    for d in range(PL):
-        q = lax.rem(p + PL - d, PL)
-        start = r * rows_w + q * w1
-        if d > 0:
-            for k in range(nz):
-                there = start + lax.rem(z + Z - k, Z) * wz if spread else start
-                i = k * (PL - 1) + d - 1
-                arrived(gw_rows(there, wz), pg_s.at[i], pg_r.at[i], p_peer(d))
-        block = gw_rows(start, w1)
-        for e in range(1, C):
-            i = d * (C - 1) + e - 1
-            send(block, block, rg_s.at[i], rg_r.at[i], r_peer(e))
-        store(block, gw_h.at[pl.ds(pl.multiple_of(start, w1), w1)])
-
+    gather_rep(0)
+    shared(full2, f2_s, f2_r)
+    store(full2, node_grad_h)
+    if T == 2:
+        gather_rep(1)
     for d in range(1, Z):
         arrived(ggz.at[lax.rem(z + Z - d, Z)], ggz_s.at[d - 1], ggz_r.at[d - 1], z_peer(d))
     ggv = ggz[0]
@@ -316,15 +358,8 @@
         ggv = ggv + ggz[k]
     gg_v[...] = ggv[:1]
     store(gg_v, gg_h)
-    shared(full2, f2_s, f2_r)
-    store(full2, node_grad_h)
-    for d in range(PL):
-        q = lax.rem(p + PL - d, PL)
-        for e in range(1, C):
-            i = d * (C - 1) + e - 1
-            there = lax.rem(r + C - e, C) * rows_w + q * w1
-            arrived(gw_rows(there, w1), rg_s.at[i], rg_r.at[i], r_peer(e))
-            store(gw_rows(there, w1), gw_h.at[pl.ds(pl.multiple_of(there, w1), w1)])
+    for t in range(T):
+        gather_end(t)
     for c in sends:
         c.wait_send()
     z_drain(nodes, x, x_s, x_r)
@@ -364,8 +399,8 @@
     group, D = nodes.shape
     ppr = Z // C
     pc = group // C
-    rows_w = 2 * D // C
-    w1 = rows_w // PL
+    T = 2 if D // C // PL % (16 * Z) == 0 else 1
+    w1 = 2 * D // C // T // PL
     spread = w1 % (16 * Z) == 0
     wz = w1 // Z if spread else w1
     V = pltpu.VMEM
@@ -382,22 +417,23 @@
         V((C, PL, pc, D), BF16), V((C - 1, PL, pc, D), BF16), V((PL - 1, pc, D), BF16),
         V((PL - 1, pc, D), BF16), V((group, D), BF16),
         V((group, D), BF16), V((2, group, D), BF16), V((2, group, D), BF16),
-        V((PL, w1, D), BF16), V((PL - 1, w1, D), BF16),
-        V((Z if spread else 1, wz, D), BF16), V((Z - 1 if spread else Z, wz, D), BF16),
+        V((T, PL, w1, D), BF16), V((T * (PL - 1), w1, D), BF16),
+        V((T, Z if spread else 1, wz, D), BF16), V((T, Z - 1 if spread else Z, wz, D), BF16),
         V((2 * D, D), BF16),
         V((8, D), F32), V((PL, 8, D), F32), V((Z, 8, D), F32), V((group, D), BF16), V((1, D), F32),
-        S((4 + ppr,)), S((3 + PL * C,)),
+        S((4 + ppr,)), S((3 + T * PL * C,)),
         *pair((PL - 1) * ppr),
         S((Z - 1,)), S((ppr,)), S((Z - 1,)), S((ppr,)),
         *pair(PL * (C - 1)), *pair(PL - 1), *pair(C - 1),
         *pair(PL * (C - 1)), *pair(PL - 1), *pair(C - 1),
-        *pair(PL - 1), *pair(Z - 1), *pair(Z - 1), *pair((PL - 1) * (w1 // wz)), *pair(PL * (C - 1)),
+        *pair(T * (PL - 1)), *pair(T * (Z - 1)), *pair(T * (Z - 1)), *pair(T * (PL - 1)),
+        *pair(T * PL * (C - 1)),
         *pair(PL - 1), *pair(Z - 1),
     ]
     H = pl.BlockSpec(memory_space=pltpu.HBM)
     M = pl.BlockSpec(memory_space=pltpu.VMEM)
     parts = pl.pallas_call(
-        functools.partial(kernel, Z, PL, C, spread),
+        functools.partial(kernel, Z, PL, C, T, spread),
         out_shape=[
             jax.ShapeDtypeStruct((group, D), BF16),
             jax.ShapeDtypeStruct((group, D), BF16),

time: 53 us -> 52.7 us (level)
  no operation moved by 1% of the time
where the time goes in v3:
time: 52.7 us; the launch traced here: 52.5 us
  Pallas kernels  51.9 us (98%)
  between operations  0.64 us (1%)
    pallas_call x1, Pallas kernels, shards(): pl.pallas_call(functools.partial(kernel, Z, PL, C, T, spread), out_shape=...  49.4 us
    pallas_call x1, Pallas kernels, shards(): pl.pallas_call(functools.partial(closing, chunks), out_shape=[jax.ShapeDt...  2.51 us

profile of v3, /device:TPU:1, one launch (start us, length us, event | category | flops | bytes accessed | tf_op | source)
XLA Modules:
  0.0 52.5 jit_solution(5804100656588628152)
XLA Ops:
  0.6 49.4 %shard_map.101 = (bf16[128,512]{1,0:T(8,128)(2,1)}, bf16[128,512]{1,0:T(8,128)(2,1)}, bf16[1024,512]{1,0:T(8,128)(2,1)}, f32[1,512]{1,0:T(1,128)}) custom-call(bf16[128,512]{1,0:T(8,128)(2,1)} %nodes_h.1, bf16[128,1024]{1,0:T(8,128)(2,1)} %adj_h.1, f32[1,512]{1,0:T(1,128)} %bitcast.2, bf16[512,512]{1,0:T(8,128)(2,1)} %w_in_h.1, bf16[512,512]{1,0:T(8,128)(2,1)} %w_out_h.1, ...), custom_call_target="tpu_custom_call" | custom-call | tf_op jit(solution)/shard_map/pallas_call | solution.py:435
  50.0 2.5 %shard_map.102 = (bf16[128,512]{1,0:T(8,128)(2,1)}, bf16[128,512]{1,0:T(8,128)(2,1)}, f32[512,512]{1,0:T(8,128)}, f32[512,512]{1,0:T(8,128)}, f32[1,512]{1,0:T(1,128)}) custom-call(bf16[128,512]{1,0:T(8,128)(2,1)} %get-tuple-element.14.node_out, bf16[128,512]{1,0:T(8,128)(2,1)} %get-tuple-element.15.node_grad, bf16[1024,512]{1,0:T(8,128)(2,1)} %get-tuple-element.16.gw, ...), custom_call_target="tpu_custom_call" | custom-call | tf_op jit(solution)/shard_map/pallas_call | solution.py:451

commit v4 on v3

--- a/solution.py
+++ b/solution.py
@@ -18,13 +18,13 @@
 
 
 def kernel(
-    Z, PL, C, T, spread,
+    Z, PL, C, T, spread, feat,
     nodes_h, adj_h, gain_ref, w_in_h, w_out_h, cot_h,
     node_out_h, node_grad_h, gw_h, gg_h,
     nodes, w_in, w_out, cot, a2, x, x2,
     part, cin, acc, pin, full, part2, cin2, acc2, pin2, full2,
     gs, lh, rh, gpart, gin, gz, gzin, gw, gg, ggp, ggz, no_v, gg_v,
-    loc, st, a_s, a_r, x_s, x_r, x2_s, x2_r,
+    loc, st, a_s, a_r, ar_s, ar_r, x_s, x_r, x2_s, x2_r,
     c_s, c_r, p_s, p_r, f_s, f_r, c2_s, c2_r, p2_s, p2_r, f2_s, f2_r,
     g_s, g_r, z_s, z_r, zg_s, zg_r, pg_s, pg_r, rg_s, rg_r,
     ggp_s, ggp_r, ggz_s, ggz_r,
@@ -40,6 +40,9 @@
     wz = w1 // Z if spread else w1
     zl = lax.rem(z, ppr)
     owner = lax.div(z, ppr) == r
+    lead = r * ppr if feat else 0
+    Dc = D // C
+    my_cols = pl.ds(pl.multiple_of(r * Dc, Dc), Dc)
     sends = []
     stores = []
 
@@ -70,10 +73,13 @@
     def arrived(dst, ss, rs, dev):
         rcopy(dst, dst, ss, rs, dev).wait_recv()
 
+    def cols_of(k):
+        return pl.ds(pl.multiple_of((lead + k) * group, group), group)
+
     own_cols = [
         pltpu.make_async_copy(
             adj_h.at[:, pl.ds(pl.multiple_of((k * PL + p) * group, group), group)],
-            a2.at[pl.ds(pl.multiple_of(p * group, group), group), pl.ds(k * group, group)],
+            a2.at[pl.ds(pl.multiple_of(p * group, group), group), cols_of(k)],
             loc.at[4 + k],
         )
         for k in range(ppr)
@@ -97,11 +103,26 @@
     loads[3].wait()
     pl.semaphore_wait(barrier, Z + PL + C - 3)
 
+    def z_rows(k):
+        return pl.ds(pl.multiple_of(k * group, group), group)
+
     def z_copies(src, buf, ss, rs):
+        if feat:
+            slot = buf.at[z_rows(z)]
+            return [
+                rcopy(src.at[:, my_cols], slot, ss.at[d - 1], rs.at[d - 1], z_peer(d))
+                for d in range(1, Z)
+            ]
         slot = buf.at[pl.ds(pl.multiple_of(zl * group, group), group)]
         return [rcopy(src, slot, ss.at[d - 1], rs.at[zl], z_peer(d)) for d in range(1, Z)]
 
     def z_start(src, buf, ss, rs):
+        if feat:
+            for c in z_copies(src, buf, ss, rs):
+                c.start()
+            buf[z_rows(z)] = src[:, my_cols]
+            return
+
         @pl.when(owner)
         def _():
             for c in z_copies(src, buf, ss, rs):
@@ -109,12 +130,22 @@
             buf[pl.ds(pl.multiple_of(zl * group, group), group)] = src[...]
 
     def z_wait(src, buf, ss, rs):
+        if feat:
+            for d in range(1, Z):
+                slot = buf.at[z_rows(lax.rem(z + Z - d, Z))]
+                arrived(slot, ss.at[d - 1], rs.at[d - 1], z_peer(d))
+            return
         for k in range(ppr):
             @pl.when(r * ppr + k != z)
             def _():
                 arrived(buf.at[pl.ds(k * group, group)], ss.at[0], rs.at[k], z_peer(1))
 
     def z_drain(src, buf, ss, rs):
+        if feat:
+            for c in z_copies(src, buf, ss, rs):
+                c.wait_send()
+            return
+
         @pl.when(owner)
         def _():
             for c in z_copies(src, buf, ss, rs):
@@ -126,7 +157,7 @@
         for k in range(ppr):
             send(
                 adj_h.at[:, pl.ds(pl.multiple_of((k * PL + q) * group, group), group)],
-                a2.at[pl.ds(pl.multiple_of(p * group, group), group), pl.ds(k * group, group)],
+                a2.at[pl.ds(pl.multiple_of(p * group, group), group), cols_of(k)],
                 a_s.at[(d - 1) * ppr + k], a_r.at[(d - 1) * ppr + k], p_peer(d),
             )
 
@@ -136,13 +167,33 @@
     loads[2].wait()
     for c in own_cols:
         c.wait()
+
+    def halves(d, e):
+        q = lax.rem(p + PL - d, PL)
+        there = pl.multiple_of(lax.rem(r + C - e, C) * ppr * group, ppr * group)
+        return a2.at[pl.ds(pl.multiple_of(q * group, group), group), pl.ds(there, ppr * group)]
+
+    def forward(d):
+        for e in range(1, C):
+            i = d * (C - 1) + e - 1
+            send(halves(d, 0), halves(d, 0), ar_s.at[i], ar_r.at[i], r_peer(e))
+
+    if feat:
+        forward(0)
     for d in range(1, PL):
         q = lax.rem(p + PL - d, PL)
         for k in range(ppr):
             arrived(
-                a2.at[pl.ds(pl.multiple_of(q * group, group), group), pl.ds(k * group, group)],
+                a2.at[pl.ds(pl.multiple_of(q * group, group), group), cols_of(k)],
                 a_s.at[(d - 1) * ppr + k], a_r.at[(d - 1) * ppr + k], p_peer(d),
             )
+        if feat:
+            forward(d)
+    if feat:
+        for d in range(PL):
+            for e in range(1, C):
+                i = d * (C - 1) + e - 1
+                arrived(halves(d, e), ar_s.at[i], ar_r.at[i], r_peer(e))
 
     order = list(range(1, PL)) + [0]
 
@@ -168,6 +219,18 @@
             accs[d - 1] = val.astype(accs.dtype)
             send(accs.at[d - 1], pins.at[d - 1], pss.at[d - 1], prs.at[d - 1], p_peer(d))
 
+    def aggregate(buf, out, ins, ss, rs, accs, pins, pss, prs):
+        if not feat:
+            partials(buf, out, ins, ss, rs)
+            return combine(out, ins, ss, rs, accs, pins, pss, prs)
+        for d in order:
+            q = lax.rem(p + d, PL)
+            val = dot(a2[pl.ds(pl.multiple_of(q * group, group), group)], buf[...])
+            if d == 0:
+                return val
+            accs[d - 1] = val.astype(accs.dtype)
+            send(accs.at[d - 1], pins.at[d - 1], pss.at[d - 1], prs.at[d - 1], p_peer(d))
+
     def finish(val, accs, pins, pss, prs):
         for d in range(1, PL):
             arrived(pins.at[d - 1], pss.at[d - 1], prs.at[d - 1], p_peer(d))
@@ -175,6 +238,8 @@
         return val
 
     def piece_of(buf, c):
+        if feat:
+            return buf.at[:, pl.ds(pl.multiple_of(c * Dc, Dc), Dc)]
         return buf.at[pl.ds(pl.multiple_of(c * pc, pc), pc)]
 
     def share(buf, ss, rs):
@@ -185,10 +250,12 @@
         for d in range(1, C):
             arrived(piece_of(buf, lax.rem(r + C - d, C)), ss.at[d - 1], rs.at[d - 1], r_peer(d))
 
-    mine = pl.ds(pl.multiple_of(r * pc, pc), pc)
+    if feat:
+        mine = (slice(None), my_cols)
+    else:
+        mine = pl.ds(pl.multiple_of(r * pc, pc), pc)
     z_wait(nodes, x, x_s, x_r)
-    partials(x, part, cin, c_s, c_r)
-    own = combine(part, cin, c_s, c_r, acc, pin, p_s, p_r)
+    own = aggregate(x, part, cin, c_s, c_r, acc, pin, p_s, p_r)
     full[mine] = finish(own, acc, pin, p_s, p_r)
     share(full, f_s, f_r)
     shared(full, f_s, f_r)
@@ -328,9 +395,8 @@
     if T == 2:
         gather_z(0)
     z_wait(gs, x2, x2_s, x2_r)
-    partials(x2, part2, cin2, c2_s, c2_r)
+    own2 = aggregate(x2, part2, cin2, c2_s, c2_r, acc2, pin2, p2_s, p2_r)
     gather_z(last)
-    own2 = combine(part2, cin2, c2_s, c2_r, acc2, pin2, p2_s, p2_r)
     for t in range(T):
         gather_plane(t)
 
@@ -399,10 +465,17 @@
     group, D = nodes.shape
     ppr = Z // C
     pc = group // C
+    feat = D // C % 128 == 0
     T = 2 if D // C // PL % (16 * Z) == 0 else 1
     w1 = 2 * D // C // T // PL
     spread = w1 % (16 * Z) == 0
     wz = w1 // Z if spread else w1
+    if feat:
+        field, piece = (Z * group, D // C), (PL - 1, group, D // C)
+        split = split_in = (8, 128)
+    else:
+        field, piece = (ppr * group, D), (PL - 1, pc, D)
+        split, split_in = (C, PL, pc, D), (C - 1, PL, pc, D)
     V = pltpu.VMEM
     S = pltpu.SemaphoreType.DMA
 
@@ -411,19 +484,18 @@
 
     scratch = [
         V((group, D), BF16), V((D, D), BF16), V((D, D), BF16), V((group, D), BF16),
-        V((PL * group, ppr * group), BF16), V((ppr * group, D), BF16), V((ppr * group, D), BF16),
-        V((C, PL, pc, D), F32), V((C - 1, PL, pc, D), F32), V((PL - 1, pc, D), F32),
-        V((PL - 1, pc, D), F32), V((group, D), F32),
-        V((C, PL, pc, D), BF16), V((C - 1, PL, pc, D), BF16), V((PL - 1, pc, D), BF16),
-        V((PL - 1, pc, D), BF16), V((group, D), BF16),
+        *([V((PL * group, Z * group), BF16)] if feat else [V((PL * group, ppr * group), BF16)]),
+        V(field, BF16), V(field, BF16),
+        V(split, F32), V(split_in, F32), V(piece, F32), V(piece, F32), V((group, D), F32),
+        V(split, BF16), V(split_in, BF16), V(piece, BF16), V(piece, BF16), V((group, D), BF16),
         V((group, D), BF16), V((2, group, D), BF16), V((2, group, D), BF16),
         V((T, PL, w1, D), BF16), V((T * (PL - 1), w1, D), BF16),
         V((T, Z if spread else 1, wz, D), BF16), V((T, Z - 1 if spread else Z, wz, D), BF16),
         V((2 * D, D), BF16),
         V((8, D), F32), V((PL, 8, D), F32), V((Z, 8, D), F32), V((group, D), BF16), V((1, D), F32),
         S((4 + ppr,)), S((3 + T * PL * C,)),
-        *pair((PL - 1) * ppr),
-        S((Z - 1,)), S((ppr,)), S((Z - 1,)), S((ppr,)),
+        *pair((PL - 1) * ppr), *pair(PL * (C - 1)),
+        S((Z - 1,)), S((Z - 1,)), S((Z - 1,)), S((Z - 1,)),
         *pair(PL * (C - 1)), *pair(PL - 1), *pair(C - 1),
         *pair(PL * (C - 1)), *pair(PL - 1), *pair(C - 1),
         *pair(T * (PL - 1)), *pair(T * (Z - 1)), *pair(T * (Z - 1)), *pair(T * (PL - 1)),
@@ -433,7 +505,7 @@
     H = pl.BlockSpec(memory_space=pltpu.HBM)
     M = pl.BlockSpec(memory_space=pltpu.VMEM)
     parts = pl.pallas_call(
-        functools.partial(kernel, Z, PL, C, T, spread),
+        functools.partial(kernel, Z, PL, C, T, spread, feat),
         out_shape=[
             jax.ShapeDtypeStruct((group, D), BF16),
             jax.ShapeDtypeStruct((group, D), BF16),

time: 52.7 us -> 48.3 us (0.917)
  Pallas kernels: 51.9 us -> 47.5 us
    pallas_call x1, Pallas kernels: 49.4 us -> 45 us  [shards(): pl.pallas_call(functools.partial(kernel, Z, PL, C, T, spread, feat), out_...]
where the time goes in v4:
time: 48.3 us; the launch traced here: 48.1 us
  Pallas kernels  47.5 us (98%)
  between operations  0.64 us (1%)
    pallas_call x1, Pallas kernels, shards(): pl.pallas_call(functools.partial(kernel, Z, PL, C, T, spread, feat), out_...  45 us
    pallas_call x1, Pallas kernels, shards(): pl.pallas_call(functools.partial(closing, chunks), out_shape=[jax.ShapeDt...  2.51 us

profile of v4, /device:TPU:1, one launch (start us, length us, event | category | flops | bytes accessed | tf_op | source)
XLA Modules:
  0.0 48.1 jit_solution(12411300621062260457)
XLA Ops:
  0.6 45.0 %shard_map.101 = (bf16[128,512]{1,0:T(8,128)(2,1)}, bf16[128,512]{1,0:T(8,128)(2,1)}, bf16[1024,512]{1,0:T(8,128)(2,1)}, f32[1,512]{1,0:T(1,128)}) custom-call(bf16[128,512]{1,0:T(8,128)(2,1)} %nodes_h.1, bf16[128,1024]{1,0:T(8,128)(2,1)} %adj_h.1, f32[1,512]{1,0:T(1,128)} %bitcast.2, bf16[512,512]{1,0:T(8,128)(2,1)} %w_in_h.1, bf16[512,512]{1,0:T(8,128)(2,1)} %w_out_h.1, ...), custom_call_target="tpu_custom_call" | custom-call | tf_op jit(solution)/shard_map/pallas_call | solution.py:507
  45.6 2.5 %shard_map.102 = (bf16[128,512]{1,0:T(8,128)(2,1)}, bf16[128,512]{1,0:T(8,128)(2,1)}, f32[512,512]{1,0:T(8,128)}, f32[512,512]{1,0:T(8,128)}, f32[1,512]{1,0:T(1,128)}) custom-call(bf16[128,512]{1,0:T(8,128)(2,1)} %get-tuple-element.14.node_out, bf16[128,512]{1,0:T(8,128)(2,1)} %get-tuple-element.15.node_grad, bf16[1024,512]{1,0:T(8,128)(2,1)} %get-tuple-element.16.gw, ...), custom_call_target="tpu_custom_call" | custom-call | tf_op jit(solution)/shard_map/pallas_call | solution.py:523

commit v5 on v4

--- a/solution.py
+++ b/solution.py
@@ -18,16 +18,16 @@
 
 
 def kernel(
-    Z, PL, C, T, spread, feat,
+    Z, PL, C, T, spread, feat, gath,
     nodes_h, adj_h, gain_ref, w_in_h, w_out_h, cot_h,
     node_out_h, node_grad_h, gw_h, gg_h,
     nodes, w_in, w_out, cot, a2, x, x2,
     part, cin, acc, pin, full, part2, cin2, acc2, pin2, full2,
-    gs, lh, rh, gpart, gin, gz, gzin, gw, gg, ggp, ggz, no_v, gg_v,
+    gs, lh, rh, gpart, gin, gz, gzin, gw, gg, ggp, ggz, no_v, gg_v, lall, rall,
     loc, st, a_s, a_r, ar_s, ar_r, x_s, x_r, x2_s, x2_r,
     c_s, c_r, p_s, p_r, f_s, f_r, c2_s, c2_r, p2_s, p2_r, f2_s, f2_r,
     g_s, g_r, z_s, z_r, zg_s, zg_r, pg_s, pg_r, rg_s, rg_r,
-    ggp_s, ggp_r, ggz_s, ggz_r,
+    ggp_s, ggp_r, ggz_s, ggz_r, l_s, l_r, ra_s, ra_r,
 ):
     g = lax.axis_index("rows")
     r = lax.axis_index("rep")
@@ -161,6 +161,34 @@
                 a_s.at[(d - 1) * ppr + k], a_r.at[(d - 1) * ppr + k], p_peer(d),
             )
 
+    def plane_copies(srcs, dst, ss, rs):
+        slot = dst.at[z_rows(p)]
+        return [rcopy(srcs(d), slot, ss.at[d - 1], rs.at[d - 1], p_peer(d)) for d in range(1, PL)]
+
+    def left_copies(k):
+        def cut(d):
+            q = lax.rem(p + d, PL)
+            return lh.at[k, :, pl.ds(pl.multiple_of(q * w1, w1), w1)]
+
+        return plane_copies(cut, lall, l_s, l_r)
+
+    def right_copies(src):
+        return plane_copies(lambda d: src, rall, ra_s, ra_r)
+
+    def begin(copies, core):
+        @pl.when(r == core)
+        def _():
+            for c in copies():
+                c.start()
+
+    def end(copies, core):
+        @pl.when(r == core)
+        def _():
+            for c in copies():
+                c.wait_send()
+
+    if gath:
+        begin(lambda: right_copies(cot_h), 1)
     loads[0].wait()
     loads[1].wait()
     grad_hidden = dot(cot[...], w_out[...], 1, 1)
@@ -265,6 +293,9 @@
     scale = lax.rsqrt(jnp.mean(summed * summed, axis=-1, keepdims=True) + 1e-05)
     normed = summed * scale
     lifted = (normed * gain).astype(BF16)
+    lh[0] = lifted
+    if gath:
+        begin(lambda: left_copies(0), 0)
     pre = dot(lifted, w_in[...])
     sigma = jax.nn.sigmoid(pre)
     hidden = (pre * sigma).astype(BF16)
@@ -286,9 +317,15 @@
         return ref[:, pl.ds(pl.multiple_of(r * rows_w, rows_w), rows_w)]
 
     lh[1] = hidden
-    if T == 2:
+    if gath:
+        begin(lambda: left_copies(1), 1)
+    elif T == 2:
         weights_start(0, columns(lh.at[1]), cot[...])
     grad_pre = (grad_hidden * sigma * (1.0 + pre * (1.0 - sigma))).astype(BF16)
+    rh[0] = grad_pre
+    rh[1] = cot[...]
+    if gath:
+        begin(lambda: right_copies(rh.at[0]), 0)
     grad_lifted = dot(grad_pre, w_in[...], 1, 1)
     grad_normed = grad_lifted * gain
     gs[...] = (
@@ -296,12 +333,12 @@
     ).astype(BF16)
     z_start(gs, x2, x2_s, x2_r)
 
-    lh[0] = lifted
-    if T == 2:
+    if gath:
+        lall[z_rows(p)] = lh[r, :, pl.ds(pl.multiple_of(p * w1, w1), w1)]
+        rall[z_rows(p)] = rh[r]
+    elif T == 2:
         weights_start(1, columns(lh.at[0]), grad_pre)
     else:
-        rh[0] = grad_pre
-        rh[1] = cot[...]
         half = C // 2
         which = lax.div(r, half)
         here = pl.multiple_of(lax.rem(r, half) * rows_w, rows_w)
@@ -317,11 +354,18 @@
         return gw.at[pl.ds(pl.multiple_of(start, count), count)]
 
     def scatter_z(t):
-        gsum = gpart[t, p].astype(F32)
-        for d in range(1, PL):
-            i = t * (PL - 1) + d - 1
-            arrived(gin.at[i], g_s.at[i], g_r.at[i], p_peer(d))
-            gsum = gsum + gin[i].astype(F32)
+        if gath:
+            for d in range(1, PL):
+                slot = z_rows(lax.rem(p + PL - d, PL))
+                arrived(lall.at[slot], l_s.at[d - 1], l_r.at[d - 1], p_peer(d))
+                arrived(rall.at[slot], ra_s.at[d - 1], ra_r.at[d - 1], p_peer(d))
+            gsum = dot(lall[...], rall[...], 0, 0)
+        else:
+            gsum = gpart[t, p].astype(F32)
+            for d in range(1, PL):
+                i = t * (PL - 1) + d - 1
+                arrived(gin.at[i], g_s.at[i], g_r.at[i], p_peer(d))
+                gsum = gsum + gin[i].astype(F32)
         if spread:
             for k in range(Z):
                 gz[t, k] = gsum[k * wz:(k + 1) * wz].astype(BF16)
@@ -351,9 +395,20 @@
             return
         here = base + z * wz
         gw[pl.ds(pl.multiple_of(here, wz), wz)] = shard.astype(BF16)
-        for d in range(1, Z):
-            i = t * (Z - 1) + d - 1
-            send(gw_rows(here, wz), gw_rows(here, wz), zg_s.at[i], zg_r.at[i], z_peer(d))
+        for c in zg_copies(t):
+            c.start()
+
+    def zg_copies(t):
+        if not spread:
+            return []
+        here = gw_rows(first_row(t, r) + p * w1 + z * wz, wz)
+        first = t * (Z - 1) - 1
+        return [rcopy(here, here, zg_s.at[first + d], zg_r.at[first + d], z_peer(d)) for d in range(1, Z)]
+
+    def pg_copies(t):
+        here = gw_rows(first_row(t, r) + p * w1, w1)
+        first = t * (PL - 1) - 1
+        return [rcopy(here, here, pg_s.at[first + d], pg_r.at[first + d], p_peer(d)) for d in range(1, PL)]
 
     def gather_plane(t):
         base = first_row(t, r) + p * w1
@@ -362,9 +417,8 @@
                 i = t * (Z - 1) + d - 1
                 there = base + lax.rem(z + Z - d, Z) * wz
                 arrived(gw_rows(there, wz), zg_s.at[i], zg_r.at[i], z_peer(d))
-        for d in range(1, PL):
-            i = t * (PL - 1) + d - 1
-            send(gw_rows(base, w1), gw_rows(base, w1), pg_s.at[i], pg_r.at[i], p_peer(d))
+        for c in pg_copies(t):
+            c.start()
 
     def keep(start):
         store(gw_rows(start, w1), gw_h.at[pl.ds(pl.multiple_of(start, w1), w1)])
@@ -392,13 +446,27 @@
     last = T - 1
     for t in range(T):
         scatter_z(t)
-    if T == 2:
+    if gath:
+        @pl.when(r == 1)
+        def _():
+            gather_z(0)
+    elif T == 2:
         gather_z(0)
     z_wait(gs, x2, x2_s, x2_r)
     own2 = aggregate(x2, part2, cin2, c2_s, c2_r, acc2, pin2, p2_s, p2_r)
-    gather_z(last)
-    for t in range(T):
-        gather_plane(t)
+    if gath:
+        @pl.when(r == 1)
+        def _():
+            gather_plane(0)
+
+        @pl.when(r == 0)
+        def _():
+            gather_z(0)
+            gather_plane(0)
+    else:
+        gather_z(last)
+        for t in range(T):
+            gather_plane(t)
 
     for d in range(1, PL):
         arrived(ggp.at[lax.rem(p + PL - d, PL)], ggp_s.at[d - 1], ggp_r.at[d - 1], p_peer(d))
@@ -428,6 +496,12 @@
         gather_end(t)
     for c in sends:
         c.wait_send()
+    for t in range(T):
+        for c in zg_copies(t) + pg_copies(t):
+            c.wait_send()
+    if gath:
+        end(lambda: left_copies(0) + right_copies(rh.at[0]), 0)
+        end(lambda: left_copies(1) + right_copies(cot_h), 1)
     z_drain(nodes, x, x_s, x_r)
     z_drain(gs, x2, x2_s, x2_r)
     for c in stores:
@@ -466,7 +540,8 @@
     ppr = Z // C
     pc = group // C
     feat = D // C % 128 == 0
-    T = 2 if D // C // PL % (16 * Z) == 0 else 1
+    gath = feat and C == 2 and D // PL % 128 == 0
+    T = 2 if D // C // PL % (16 * Z) == 0 and not gath else 1
     w1 = 2 * D // C // T // PL
     spread = w1 % (16 * Z) == 0
     wz = w1 // Z if spread else w1
@@ -493,6 +568,7 @@
         V((T, Z if spread else 1, wz, D), BF16), V((T, Z - 1 if spread else Z, wz, D), BF16),
         V((2 * D, D), BF16),
         V((8, D), F32), V((PL, 8, D), F32), V((Z, 8, D), F32), V((group, D), BF16), V((1, D), F32),
+        V((PL * group, w1 if gath else 128), BF16), V((PL * group, D), BF16),
         S((4 + ppr,)), S((3 + T * PL * C,)),
         *pair((PL - 1) * ppr), *pair(PL * (C - 1)),
         S((Z - 1,)), S((Z - 1,)), S((Z - 1,)), S((Z - 1,)),
@@ -500,12 +576,12 @@
         *pair(PL * (C - 1)), *pair(PL - 1), *pair(C - 1),
         *pair(T * (PL - 1)), *pair(T * (Z - 1)), *pair(T * (Z - 1)), *pair(T * (PL - 1)),
         *pair(T * PL * (C - 1)),
-        *pair(PL - 1), *pair(Z - 1),
+        *pair(PL - 1), *pair(Z - 1), *pair(PL - 1), *pair(PL - 1),
     ]
     H = pl.BlockSpec(memory_space=pltpu.HBM)
     M = pl.BlockSpec(memory_space=pltpu.VMEM)
     parts = pl.pallas_call(
-        functools.partial(kernel, Z, PL, C, T, spread, feat),
+        functools.partial(kernel, Z, PL, C, T, spread, feat, gath),
         out_shape=[
             jax.ShapeDtypeStruct((group, D), BF16),
             jax.ShapeDtypeStruct((group, D), BF16),

time: 48.3 us -> 50.1 us (1.037)
  Pallas kernels: 47.5 us -> 49.2 us
    pallas_call x1, Pallas kernels: 45 us -> 46.7 us  [shards(): pl.pallas_call(functools.partial(kernel, Z, PL, C, T, spread, feat, gath)...]
where the time goes in v5:
time: 50.1 us; the launch traced here: 49.9 us
  Pallas kernels  49.2 us (98%)
  between operations  0.64 us (1%)
    pallas_call x1, Pallas kernels, shards(): pl.pallas_call(functools.partial(kernel, Z, PL, C, T, spread, feat, gath)...  46.7 us
    pallas_call x1, Pallas kernels, shards(): pl.pallas_call(functools.partial(closing, chunks), out_shape=[jax.ShapeDt...  2.51 us

profile of v5, /device:TPU:1, one launch (start us, length us, event | category | flops | bytes accessed | tf_op | source)
XLA Modules:
  0.0 49.9 jit_solution(5982540102558482066)
XLA Ops:
  0.6 46.7 %shard_map.101 = (bf16[128,512]{1,0:T(8,128)(2,1)}, bf16[128,512]{1,0:T(8,128)(2,1)}, bf16[1024,512]{1,0:T(8,128)(2,1)}, f32[1,512]{1,0:T(1,128)}) custom-call(bf16[128,512]{1,0:T(8,128)(2,1)} %nodes_h.1, bf16[128,1024]{1,0:T(8,128)(2,1)} %adj_h.1, f32[1,512]{1,0:T(1,128)} %bitcast.2, bf16[512,512]{1,0:T(8,128)(2,1)} %w_in_h.1, bf16[512,512]{1,0:T(8,128)(2,1)} %w_out_h.1, ...), custom_call_target="tpu_custom_call" | custom-call | tf_op jit(solution)/shard_map/pallas_call | solution.py:583
  47.4 2.5 %shard_map.102 = (bf16[128,512]{1,0:T(8,128)(2,1)}, bf16[128,512]{1,0:T(8,128)(2,1)}, f32[512,512]{1,0:T(8,128)}, f32[512,512]{1,0:T(8,128)}, f32[1,512]{1,0:T(1,128)}) custom-call(bf16[128,512]{1,0:T(8,128)(2,1)} %get-tuple-element.14.node_out, bf16[128,512]{1,0:T(8,128)(2,1)} %get-tuple-element.15.node_grad, bf16[1024,512]{1,0:T(8,128)(2,1)} %get-tuple-element.16.gw, ...), custom_call_target="tpu_custom_call" | custom-call | tf_op jit(solution)/shard_map/pallas_call | solution.py:599

commit v6 on v5

--- a/solution.py
+++ b/solution.py
@@ -187,8 +187,6 @@
             for c in copies():
                 c.wait_send()
 
-    if gath:
-        begin(lambda: right_copies(cot_h), 1)
     loads[0].wait()
     loads[1].wait()
     grad_hidden = dot(cot[...], w_out[...], 1, 1)
@@ -222,6 +220,9 @@
             for e in range(1, C):
                 i = d * (C - 1) + e - 1
                 arrived(halves(d, e), ar_s.at[i], ar_r.at[i], r_peer(e))
+
+    if gath:
+        begin(lambda: right_copies(cot_h), 1)
 
     order = list(range(1, PL)) + [0]
 

time: 50.1 us -> 51.7 us (1.032)
  Pallas kernels: 49.2 us -> 50.9 us
    pallas_call x1, Pallas kernels: 46.7 us -> 48.4 us  [shards(): pl.pallas_call(functools.partial(kernel, Z, PL, C, T, spread, feat, gath)...]
where the time goes in v6:
time: 51.7 us; the launch traced here: 51.5 us
  Pallas kernels  50.9 us (98%)
  between operations  0.64 us (1%)
    pallas_call x1, Pallas kernels, shards(): pl.pallas_call(functools.partial(kernel, Z, PL, C, T, spread, feat, gath)...  48.4 us
    pallas_call x1, Pallas kernels, shards(): pl.pallas_call(functools.partial(closing, chunks), out_shape=[jax.ShapeDt...  2.51 us

profile of v6, /device:TPU:1, one launch (start us, length us, event | category | flops | bytes accessed | tf_op | source)
XLA Modules:
  0.0 51.5 jit_solution(1625124821607618897)
XLA Ops:
  0.6 48.4 %shard_map.101 = (bf16[128,512]{1,0:T(8,128)(2,1)}, bf16[128,512]{1,0:T(8,128)(2,1)}, bf16[1024,512]{1,0:T(8,128)(2,1)}, f32[1,512]{1,0:T(1,128)}) custom-call(bf16[128,512]{1,0:T(8,128)(2,1)} %nodes_h.1, bf16[128,1024]{1,0:T(8,128)(2,1)} %adj_h.1, f32[1,512]{1,0:T(1,128)} %bitcast.2, bf16[512,512]{1,0:T(8,128)(2,1)} %w_in_h.1, bf16[512,512]{1,0:T(8,128)(2,1)} %w_out_h.1, ...), custom_call_target="tpu_custom_call" | custom-call | tf_op jit(solution)/shard_map/pallas_call | solution.py:584
  49.0 2.5 %shard_map.102 = (bf16[128,512]{1,0:T(8,128)(2,1)}, bf16[128,512]{1,0:T(8,128)(2,1)}, f32[512,512]{1,0:T(8,128)}, f32[512,512]{1,0:T(8,128)}, f32[1,512]{1,0:T(1,128)}) custom-call(bf16[128,512]{1,0:T(8,128)(2,1)} %get-tuple-element.14.node_out, bf16[128,512]{1,0:T(8,128)(2,1)} %get-tuple-element.15.node_grad, bf16[1024,512]{1,0:T(8,128)(2,1)} %get-tuple-element.16.gw, ...), custom_call_target="tpu_custom_call" | custom-call | tf_op jit(solution)/shard_map/pallas_call | solution.py:600

commit v7 on v4

--- a/solution.py
+++ b/solution.py
@@ -286,8 +286,6 @@
         return ref[:, pl.ds(pl.multiple_of(r * rows_w, rows_w), rows_w)]
 
     lh[1] = hidden
-    if T == 2:
-        weights_start(0, columns(lh.at[1]), cot[...])
     grad_pre = (grad_hidden * sigma * (1.0 + pre * (1.0 - sigma))).astype(BF16)
     grad_lifted = dot(grad_pre, w_in[...], 1, 1)
     grad_normed = grad_lifted * gain
@@ -298,6 +296,7 @@
 
     lh[0] = lifted
     if T == 2:
+        weights_start(0, columns(lh.at[1]), cot[...])
         weights_start(1, columns(lh.at[0]), grad_pre)
     else:
         rh[0] = grad_pre
@@ -486,7 +485,7 @@
         V((group, D), BF16), V((D, D), BF16), V((D, D), BF16), V((group, D), BF16),
         *([V((PL * group, Z * group), BF16)] if feat else [V((PL * group, ppr * group), BF16)]),
         V(field, BF16), V(field, BF16),
-        V(split, F32), V(split_in, F32), V(piece, F32), V(piece, F32), V((group, D), F32),
+        V(split, F32), V(split_in, F32), V(piece, BF16), V(piece, BF16), V((group, D), F32),
         V(split, BF16), V(split_in, BF16), V(piece, BF16), V(piece, BF16), V((group, D), BF16),
         V((group, D), BF16), V((2, group, D), BF16), V((2, group, D), BF16),
         V((T, PL, w1, D), BF16), V((T * (PL - 1), w1, D), BF16),

time: 48.3 us -> 45.7 us (0.946)
  Pallas kernels: 47.5 us -> 44.9 us
    pallas_call x1, Pallas kernels: 45 us -> 42.4 us  [shards(): pl.pallas_call(functools.partial(kernel, Z, PL, C, T, spread, feat), out_...]
where the time goes in v7:
time: 45.7 us; the launch traced here: 45.6 us
  Pallas kernels  44.9 us (98%)
  between operations  0.64 us (1%)
    pallas_call x1, Pallas kernels, shards(): pl.pallas_call(functools.partial(kernel, Z, PL, C, T, spread, feat), out_...  42.4 us
    pallas_call x1, Pallas kernels, shards(): pl.pallas_call(functools.partial(closing, chunks), out_shape=[jax.ShapeDt...  2.51 us

profile of v7, /device:TPU:1, one launch (start us, length us, event | category | flops | bytes accessed | tf_op | source)
XLA Modules:
  0.0 45.6 jit_solution(13562785865898780986)
XLA Ops:
  0.6 42.4 %shard_map.101 = (bf16[128,512]{1,0:T(8,128)(2,1)}, bf16[128,512]{1,0:T(8,128)(2,1)}, bf16[1024,512]{1,0:T(8,128)(2,1)}, f32[1,512]{1,0:T(1,128)}) custom-call(bf16[128,512]{1,0:T(8,128)(2,1)} %nodes_h.1, bf16[128,1024]{1,0:T(8,128)(2,1)} %adj_h.1, f32[1,512]{1,0:T(1,128)} %bitcast.2, bf16[512,512]{1,0:T(8,128)(2,1)} %w_in_h.1, bf16[512,512]{1,0:T(8,128)(2,1)} %w_out_h.1, ...), custom_call_target="tpu_custom_call" | custom-call | tf_op jit(solution)/shard_map/pallas_call | solution.py:506
  43.1 2.5 %shard_map.102 = (bf16[128,512]{1,0:T(8,128)(2,1)}, bf16[128,512]{1,0:T(8,128)(2,1)}, f32[512,512]{1,0:T(8,128)}, f32[512,512]{1,0:T(8,128)}, f32[1,512]{1,0:T(1,128)}) custom-call(bf16[128,512]{1,0:T(8,128)(2,1)} %get-tuple-element.14.node_out, bf16[128,512]{1,0:T(8,128)(2,1)} %get-tuple-element.15.node_grad, bf16[1024,512]{1,0:T(8,128)(2,1)} %get-tuple-element.16.gw, ...), custom_call_target="tpu_custom_call" | custom-call | tf_op jit(solution)/shard_map/pallas_call | solution.py:522

commit v8 on v7

--- a/solution.py
+++ b/solution.py
@@ -389,12 +389,12 @@
                 keep(start)
 
     last = T - 1
-    for t in range(T):
-        scatter_z(t)
-    if T == 2:
-        gather_z(0)
+    scatter_z(0)
     z_wait(gs, x2, x2_s, x2_r)
     own2 = aggregate(x2, part2, cin2, c2_s, c2_r, acc2, pin2, p2_s, p2_r)
+    if T == 2:
+        scatter_z(1)
+        gather_z(0)
     gather_z(last)
     for t in range(T):
         gather_plane(t)

time: 45.7 us -> 45.8 us (level)
  no operation moved by 1% of the time
where the time goes in v8:
time: 45.8 us; the launch traced here: 45.6 us
  Pallas kernels  44.9 us (98%)
  between operations  0.64 us (1%)
    pallas_call x1, Pallas kernels, shards(): pl.pallas_call(functools.partial(kernel, Z, PL, C, T, spread, feat), out_...  42.4 us
    pallas_call x1, Pallas kernels, shards(): pl.pallas_call(functools.partial(closing, chunks), out_shape=[jax.ShapeDt...  2.51 us

profile of v8, /device:TPU:1, one launch (start us, length us, event | category | flops | bytes accessed | tf_op | source)
XLA Modules:
  0.0 45.6 jit_solution(10788456616406947183)
XLA Ops:
  0.6 42.4 %shard_map.101 = (bf16[128,512]{1,0:T(8,128)(2,1)}, bf16[128,512]{1,0:T(8,128)(2,1)}, bf16[1024,512]{1,0:T(8,128)(2,1)}, f32[1,512]{1,0:T(1,128)}) custom-call(bf16[128,512]{1,0:T(8,128)(2,1)} %nodes_h.1, bf16[128,1024]{1,0:T(8,128)(2,1)} %adj_h.1, f32[1,512]{1,0:T(1,128)} %bitcast.2, bf16[512,512]{1,0:T(8,128)(2,1)} %w_in_h.1, bf16[512,512]{1,0:T(8,128)(2,1)} %w_out_h.1, ...), custom_call_target="tpu_custom_call" | custom-call | tf_op jit(solution)/shard_map/pallas_call | solution.py:506
  43.1 2.5 %shard_map.102 = (bf16[128,512]{1,0:T(8,128)(2,1)}, bf16[128,512]{1,0:T(8,128)(2,1)}, f32[512,512]{1,0:T(8,128)}, f32[512,512]{1,0:T(8,128)}, f32[1,512]{1,0:T(1,128)}) custom-call(bf16[128,512]{1,0:T(8,128)(2,1)} %get-tuple-element.14.node_out, bf16[128,512]{1,0:T(8,128)(2,1)} %get-tuple-element.15.node_grad, bf16[1024,512]{1,0:T(8,128)(2,1)} %get-tuple-element.16.gw, ...), custom_call_target="tpu_custom_call" | custom-call | tf_op jit(solution)/shard_map/pallas_call | solution.py:522
